TPU v7x, 32 devices: a whole 2x2x4 slice. The times are simulated.
32 devices in a mesh: st: 8 (over z, x), ch: 4 (over y, core).
Axes of the slice: x: 2, y: 2, z: 4, core: 2. Of those that a mesh axis runs over, the one named last changes fastest.
Arguments:
- waveform: bfloat16 [256, 3, 8704], P('st'), may hold values from -500 to 500
- templates: bfloat16 [416, 32, 512], P('st', 'ch'), may hold values from -50 to 50
- block_of: int32 [4, 416, 2], P('ch'), may hold values from 0 to 7, all different within a row; in each aligned block of 52 rows (0 to 51, 52 to 103, ..., all dimensions but the last counted through in order) at most 17 rows name the same one
- trace_of: int32 [4, 8, 8, 4], P('ch'), may hold values from 0 to 95
Outputs:
- detection: float32 [416, 8192], P('st', 'ch')
Inputs may be any that keep to these rules, and one draw needn't show every extreme that they name: `block_of`: a row names two different station blocks; among the 52 templates of one owner (aligned blocks of the template dimension) in one group, no station block is named by more than 17 templates, and some station block is named by exactly 17.
All inputs are finite; a program needn't handle non-finite values.
Results may differ from a plain program's by a relative error of at most 0.00035.
Values may be sent and summed in bfloat16 or wider, within the bound.
A program may use at most 192 MiB of HBM per device.

v0:
```python
import functools

import jax
import jax.numpy as jnp
from jax import lax
from jax.experimental import pallas as pl
from jax.experimental.pallas import tpu as pltpu
from jax.sharding import PartitionSpec as P

EPSILON = 1e-05
SHIFTS = 32
GROUP = 4


def correlate_kernel(
    dims, start_ref, order_ref, gain_ref, lanes_ref, filters_ref, out_ref, hankel, skewed, scale
):
    templates, pairs, half, taps, cols, depth = dims
    block = pl.program_id(0)
    width = lanes_ref.shape[-1]

    @pl.when(block == 0)
    def _():
        out_ref[...] = jnp.zeros_like(out_ref)
        hankel[...] = jnp.zeros_like(hankel)

    row = lax.broadcasted_iota(jnp.int32, (SHIFTS, width), 0)
    blocks_per_tap = taps // SHIFTS

    def ahead(x, by):
        return pltpu.roll(x, (x.shape[1] - by) % x.shape[1], 1)

    for c in range(half):
        lanes = lanes_ref[0, c].astype(jnp.float32)
        for q in range(blocks_per_tap + 1):
            moved = lanes if q == 0 else ahead(lanes, q)
            hankel[c, q * SHIFTS : (q + 1) * SHIFTS, :] = moved[:, :cols].astype(jnp.bfloat16)
        squares = lanes * lanes
        prefix, suffix = squares, squares
        step = 1
        while step < SHIFTS:
            prefix = prefix + jnp.where(row >= step, pltpu.roll(prefix, step, 0), 0.0)
            suffix = suffix + jnp.where(
                row < SHIFTS - step, pltpu.roll(suffix, SHIFTS - step, 0), 0.0
            )
            step *= 2
        before = jnp.where(row >= 1, pltpu.roll(prefix, 1, 0), 0.0)
        total = jnp.broadcast_to(jnp.sum(squares, axis=0, keepdims=True), (SHIFTS, width))
        middle, at, power, run = jnp.zeros_like(total), 1, 1, total
        count = blocks_per_tap - 1
        while count:
            if count & 1:
                middle = middle + ahead(run, at)
                at += power
            count >>= 1
            if count:
                run = run + ahead(run, power)
                power *= 2
        energy = suffix + middle + ahead(before, blocks_per_tap)
        scale[c] = lax.rsqrt(energy[:, :cols] / taps + EPSILON)

    first, last = start_ref[block], start_ref[block + 1]

    def chunk(number, carry):
        base = first + number * GROUP
        for g in range(GROUP):
            pair = order_ref[base + g]
            rows = filters_ref[pair]
            for c in range(half):
                spread = jnp.broadcast_to(rows[c : c + 1], (SHIFTS, depth))
                spread = pltpu.roll(spread, 0, 1, stride=1, stride_axis=0)
                skewed[c, g * SHIFTS : (g + 1) * SHIFTS, :] = spread.astype(jnp.bfloat16)
        totals = [None] * GROUP
        for c in range(half):
            raw = jnp.dot(skewed[c], hankel[c], preferred_element_type=jnp.float32)
            for g in range(GROUP):
                pair = order_ref[base + g]
                term = raw[g * SHIFTS : (g + 1) * SHIFTS] * (scale[c] * gain_ref[pair * half + c])
                totals[g] = term if c == 0 else totals[g] + term
        for g in range(GROUP):
            place = jnp.where(base + g < last, lax.div(order_ref[base + g], 2), templates)
            out_ref[place] += totals[g]
        return carry

    lax.fori_loop(0, lax.div(last - first + GROUP - 1, GROUP), chunk, 0)


def correlate(arrived, filters, sources):
    blocks, half, window = arrived.shape
    templates = filters.shape[0]
    taps = filters.shape[2]
    pairs = templates * 2
    lags = window - taps
    cols = lags // SHIFTS
    used = window // SHIFTS
    width = -(-used // 128) * 128
    depth = -(-(taps + SHIFTS) // 128) * 128

    lanes = arrived.reshape(blocks, half, used, SHIFTS).transpose(0, 1, 3, 2)
    lanes = jnp.pad(lanes, ((0, 0), (0, 0), (0, 0), (0, width - used)))
    wide = filters.astype(jnp.float32)
    gain = 1.0 / (taps * jnp.sqrt(jnp.mean(wide * wide, axis=2) + EPSILON))
    padded = jnp.pad(wide.reshape(pairs, half, taps), ((0, 0), (0, 0), (0, depth - taps)))

    named = sources.reshape(pairs)
    ids = jnp.arange(pairs, dtype=jnp.int32)
    ahead = (named[None, :] < named[:, None]) | (
        (named[None, :] == named[:, None]) & (ids[None, :] < ids[:, None])
    )
    place = jnp.sum(ahead.astype(jnp.int32), axis=1)
    spots = jnp.arange(pairs + GROUP, dtype=jnp.int32)
    order = jnp.sum(jnp.where(place[None, :] == spots[:, None], ids[None, :], 0), axis=1)
    edges = jnp.arange(blocks + 1, dtype=jnp.int32)
    start = jnp.sum((named[None, :] < edges[:, None]).astype(jnp.int32), axis=1)

    dims = (templates, pairs, half, taps, cols, depth)
    smem = pl.BlockSpec(memory_space=pltpu.SMEM)
    return pl.pallas_call(
        functools.partial(correlate_kernel, dims),
        grid=(blocks,),
        out_shape=jax.ShapeDtypeStruct((templates + 1, SHIFTS, cols), jnp.float32),
        in_specs=[
            smem,
            smem,
            smem,
            pl.BlockSpec((1, half, SHIFTS, width), lambda b: (b, 0, 0, 0)),
            pl.BlockSpec((pairs, half, depth), lambda b: (0, 0, 0)),
        ],
        out_specs=pl.BlockSpec((templates + 1, SHIFTS, cols), lambda b: (0, 0, 0)),
        scratch_shapes=[
            pltpu.VMEM((half, depth, cols), jnp.bfloat16),
            pltpu.VMEM((half, GROUP * SHIFTS, depth), jnp.bfloat16),
            pltpu.VMEM((half, SHIFTS, cols), jnp.float32),
        ],
        compiler_params=pltpu.CompilerParams(vmem_limit_bytes=40 * 1024 * 1024),
        name="correlate",
    )(start, order, gain.reshape(-1), lanes, padded)


def per_device(waveform, templates, block_of, trace_of):
    own_index = lax.axis_index("st")
    station_count = lax.axis_size("st")
    own_templates = templates.shape[0]
    group_chans = templates.shape[1]
    half_chans = group_chans // 2
    window = waveform.shape[2]
    local_rows = waveform.reshape(-1, window)
    sources = block_of[0].reshape(station_count, own_templates, 2)
    own_sources = lax.dynamic_index_in_dim(sources, own_index, 0, keepdims=False)
    wanted = lax.dynamic_index_in_dim(trace_of[0], own_index, 1, keepdims=False)
    source_rows = jnp.take(local_rows, wanted.reshape(-1), axis=0)
    arrived = lax.all_to_all(
        source_rows.reshape(station_count, half_chans, window),
        "st",
        split_axis=0,
        concat_axis=0,
        tiled=True,
    )
    sums = correlate(arrived, templates, own_sources)[:own_templates]
    partial_value = sums.transpose(0, 2, 1).reshape(own_templates, -1)
    return lax.psum_scatter(partial_value, "ch", scatter_dimension=1, tiled=True)


def solution(mesh):
    in_specs = (
        P("st", None, None),
        P("st", "ch", None),
        P("ch", None, None),
        P("ch", None, None, None),
    )
    out_specs = P("st", "ch")
    return jax.shard_map(
        per_device, mesh=mesh, in_specs=in_specs, out_specs=out_specs, check_vma=False
    )
```

profile of v0, /device:TPU:0, one launch (start us, length us, event | category | flops | bytes accessed | tf_op | source)
XLA Modules:
  0.0 127.4 jit_solution(6603605924141172541)
XLA Ops:
  6.5 1.0 fusion.3
  7.8 4.3 %copy.46 = bf16[32,3,8704]{2,1,0:T(4,128)(2,1)} copy(bf16[32,3,8704]{2,0,1:T(8,128)(2,1)} %param.4) | data formatting | bytes 3342336 | tf_op args[0]
  12.1 3.2 %reshape.76 = bf16[96,8704]{1,0:T(8,128)(2,1)S(1)} reshape(bf16[32,3,8704]{2,1,0:T(4,128)(2,1)} %copy.46) | data formatting | bytes 3342336 | tf_op jit(solution)/shard_map/reshape | solution.py:147
  15.4 0.9 gather_fusion
  16.3 0.1 gather.7
  16.4 1.1 broadcast_select_fusion
  17.5 7.3 %all-to-all-start = ((bf16[8,4,8704]{2,1,0:T(4,128)(2,1)}), bf16[8,4,8704]{2,1,0:T(4,128)(2,1)}, u32[]{:S(2)}, u32[]{:S(2)}) async-start(bf16[8,4,8704]{2,1,0:T(4,128)(2,1)} %broadcast_select_fusion), calls=%async_computation | async-start | bytes 1114112 | tf_op jit(solution)/shard_map/all_to_all | solution.py:152
  24.9 0.1 copy.53
  25.0 0.1 lt.70
  25.2 0.3 reshape.79
  25.5 0.2 multiply_reduce_fusion
  25.9 0.2 pad.9.filters_ref
  26.1 0.1 convert_reduce_fusion.1.start_ref
  26.2 0.2 convert_reduce_fusion
  26.4 0.1 select_reduce_fusion.order_ref
  26.5 13.6 %all-to-all-done = bf16[8,4,8704]{2,1,0:T(4,128)(2,1)} async-done(((bf16[8,4,8704]{2,1,0:T(4,128)(2,1)}), bf16[8,4,8704]{2,1,0:T(4,128)(2,1)}, u32[]{:S(2)}, u32[]{:S(2)}) %all-to-all-start) | async-done | bytes 557088 | tf_op jit(solution)/shard_map/all_to_all | solution.py:152
  40.1 2.9 %reshape.91 = bf16[8,4,272,32]{3,2,1,0:T(8,128)(2,1)S(1)} reshape(bf16[8,4,8704]{2,1,0:T(4,128)(2,1)} %all-to-all-done) | data formatting | bytes 1114112 | tf_op jit(solution)/shard_map/reshape | solution.py:99
  43.0 1.8 %copy.48 = bf16[8,4,272,32]{2,3,1,0:T(8,128)(2,1)} copy(bf16[8,4,272,32]{3,2,1,0:T(8,128)(2,1)S(1)} %reshape.91) | data formatting | bytes 1114112 | tf_op jit(solution)/shard_map/reshape | solution.py:99
  44.8 1.2 pad.8.lanes_ref
  46.0 24.1 %correlate.1 = f32[53,32,256]{2,1,0:T(8,128)S(1)} custom-call(s32[9]{0:T(128)S(1)} %convert_reduce_fusion.1.start_ref, s32[108]{0:T(128)S(1)} %select_reduce_fusion.order_ref, f32[416]{0:T(512)S(1)} %reshape.82.gain_ref, bf16[8,4,32,384]{3,2,1,0:T(8,128)(2,1)S(1)} %pad.8.lanes_ref, f32[104,4,640]{2,1,0:T(4,128)S(1)} %pad.9.filters_ref), custom_call_target="tpu_custom_call" | custom-call | tf_op jit(solution)/shard_map/correlate/pallas_call | solution.py:118
  70.2 0.1 slice_bitcast_fusion
  70.3 4.5 %copy.49 = f32[52,256,32]{0,2,1:T(8,128)} copy(f32[52,256,32]{1,2,0:T(8,128)S(1)} %slice_bitcast_fusion) | data formatting | bytes 3407872 | tf_op jit(solution)/shard_map/transpose | solution.py:160
  74.9 43.3 %reduce-scatter.2.cloned.1.call-done = f32[52,2048]{0,1:T(8,128)} async-done(((f32[52,8192]{0,1:T(8,128)}), f32[52,2048]{0,1:T(8,128)}) %reduce-scatter.2.cloned.1.call-update) | async-done | bytes 426000 | tf_op jit(solution)/shard_map/reduce_scatter | solution.py:161
  118.2 2.3 %copy.50 = f32[52,2048]{1,0:T(8,128)} copy(f32[52,2048]{0,1:T(8,128)} %reduce-scatter.2.cloned.1.call-done) | data formatting | bytes 851968 | tf_op jit(solution)/shard_map/reduce_scatter | solution.py:161
  (18 shorter events, 0.7 us)
Async XLA Ops:
  16.3 8.6 %copy-start.1 = (s32[1,416,2]{1,2,0:T(2,128)S(1)}, s32[1,416,2]{1,2,0:T(2,128)}, u32[]{:S(2)}) copy-start(s32[1,416,2]{1,2,0:T(2,128)} %param.6) | copy-start | bytes 9988
  16.3 8.9 %copy-start = (bf16[52,8,512]{2,1,0:T(8,128)(2,1)S(1)}, bf16[52,8,512]{2,1,0:T(8,128)(2,1)}, u32[]{:S(2)}) copy-start(bf16[52,8,512]{2,1,0:T(8,128)(2,1)} %param.5) | copy-start | bytes 1277956
  17.5 22.5 %all-to-all-start = ((bf16[8,4,8704]{2,1,0:T(4,128)(2,1)}), bf16[8,4,8704]{2,1,0:T(4,128)(2,1)}, u32[]{:S(2)}, u32[]{:S(2)}) async-start(bf16[8,4,8704]{2,1,0:T(4,128)(2,1)} %broadcast_select_fusion), calls=%async_computation | async-start | bytes 1114112 | tf_op jit(solution)/shard_map/all_to_all | solution.py:152
  24.8 93.4 %reduce-scatter.2.cloned.1.call-start = ((), (), s32[]{:S(2)}) async-start(), calls=%async_computation.2 | async-start | bytes 5242880 | tf_op jit(solution)/shard_map/reduce_scatter | solution.py:161
Sparse Core Ops, SparseCore 0:
  75.0 43.1 reduce-scatter.1
where the time goes:
time: 128 us; the launch traced here: 127 us
  waiting for transfers between devices  56.9 us (44%)
  Pallas kernels  24.1 us (19%)
  local copies, waits for them, and re-layouts  23.8 us (19%)
  between operations  13.5 us (11%)
  starting transfers between devices  7.29 us (6%)
  other arithmetic  1.7 us (1%)
    reduce_scatter x1, waiting for transfers between devices, per_device(): lax.psum_scatter(partial_value, 'ch', scatter_dimension=1, tiled=True)  43.3 us
    pallas_call x1, Pallas kernels, correlate(): pl.pallas_call(functools.partial(correlate_kernel, dims), grid=(blocks,),...  24.1 us
    all_to_all x1, waiting for transfers between devices, per_device(): lax.all_to_all(source_rows.reshape(station_count, half_chans, window), 's...  13.6 us
    all_to_all x1, starting transfers between devices, per_device(): lax.all_to_all(source_rows.reshape(station_count, half_chans, window), 's...  7.25 us
    reshape x2, local copies, waits for them, and re-layouts, correlate(): lanes = arrived.reshape(blocks, half, used, SHIFTS).transpose(0, 1, 3, 2)  4.72 us
    transpose x2, local copies, waits for them, and re-layouts, per_device(): partial_value = sums.transpose(0, 2, 1).reshape(own_templates, -1)  4.65 us
    unnamed x6, local copies, waits for them, and re-layouts  4.39 us
    reshape x1, local copies, waits for them, and re-layouts, per_device(): local_rows = waveform.reshape(-1, window)  3.23 us
  transfers between devices with their start and end apart: 2, of which 2 were waited for; matrix products, arithmetic and copies ran while one was open for 1% of the time, Pallas kernels for 0%

commit v1 on v0

v1 whole, which is shorter than its diff:
```python
import functools

import jax
import jax.numpy as jnp
from jax import lax
from jax.experimental import pallas as pl
from jax.experimental.pallas import tpu as pltpu
from jax.sharding import PartitionSpec as P

EPSILON = 1e-05
SHIFTS = 32
LANES = 128
GROUP = 4


def correlate_kernel(
    dims,
    me_ref,
    start_ref,
    order_ref,
    gain_ref,
    lanes_ref,
    filters_ref,
    keep_ref,
    send_ref,
    totals_ref,
    padded,
    hankel,
    skewed,
    scale,
    turned,
):
    templates, half, taps, used, depth, parts = dims
    block = pl.program_id(0)

    @pl.when(block == 0)
    def _():
        totals_ref[...] = jnp.zeros_like(totals_ref)
        hankel[...] = jnp.zeros_like(hankel)
        padded[...] = jnp.zeros_like(padded)

    row = lax.broadcasted_iota(jnp.int32, (LANES, LANES), 0)
    low = lax.broadcasted_iota(jnp.int32, (SHIFTS, LANES), 1) < LANES // 2
    whole = taps // LANES
    splits = LANES // SHIFTS

    def ahead(x, by):
        by = (LANES - by) % LANES
        return x if by == 0 else pltpu.roll(x, by, 1)

    def strip(x, m):
        at = (m % splits) * SHIFTS
        return x[at : at + SHIFTS]

    def joined(x, m):
        left = ahead(strip(x, m), m // splits)
        right = ahead(strip(x, m + 1), (m + 1) // splits - LANES // 2)
        return jnp.where(low, left, right)

    for c in range(half):
        padded[:used, :] = lanes_ref[0, c].astype(jnp.float32)
        lanes = padded[...].T
        steps = taps // SHIFTS + 1
        for m in range(steps + 2):
            pair = joined(lanes, m).astype(jnp.bfloat16)
            if m < steps:
                hankel[c, m * SHIFTS : (m + 1) * SHIFTS, :LANES] = pair
            if m >= 2:
                hankel[c, (m - 2) * SHIFTS : (m - 1) * SHIFTS, LANES:] = pair
        squares = lanes * lanes
        prefix, suffix = squares, squares
        step = 1
        while step < LANES:
            prefix = prefix + jnp.where(row >= step, pltpu.roll(prefix, step, 0), 0.0)
            suffix = suffix + jnp.where(
                row < LANES - step, pltpu.roll(suffix, LANES - step, 0), 0.0
            )
            step *= 2
        before = jnp.where(row >= 1, pltpu.roll(prefix, 1, 0), 0.0)
        total = jnp.sum(squares, axis=0, keepdims=True)
        middle = jnp.zeros_like(total)
        for by in range(1, whole):
            middle = middle + ahead(total, by)
        energy = suffix + middle + ahead(before, whole)
        root = lax.rsqrt(energy / taps + EPSILON)
        scale[c, :, :LANES] = joined(root, 0)
        scale[c, :, LANES:] = joined(root, 2)

    first, last = start_ref[block], start_ref[block + 1]

    def chunk(number, carry):
        base = first + number * GROUP
        for g in range(GROUP):
            pair = order_ref[base + g]
            rows = filters_ref[pair]
            for c in range(half):
                spread = jnp.broadcast_to(rows[c : c + 1], (SHIFTS, depth))
                spread = pltpu.roll(spread, 0, 1, stride=1, stride_axis=0)
                skewed[c, g * SHIFTS : (g + 1) * SHIFTS, :] = spread.astype(jnp.bfloat16)
        totals = [None] * GROUP
        for c in range(half):
            raw = jnp.dot(skewed[c], hankel[c], preferred_element_type=jnp.float32)
            for g in range(GROUP):
                pair = order_ref[base + g]
                term = raw[g * SHIFTS : (g + 1) * SHIFTS] * (scale[c] * gain_ref[pair * half + c])
                totals[g] = term if c == 0 else totals[g] + term
        for g in range(GROUP):
            place = jnp.where(base + g < last, lax.div(order_ref[base + g], 2), templates)
            totals_ref[place] += totals[g]
        return carry

    lax.fori_loop(0, lax.div(last - first + GROUP - 1, GROUP), chunk, 0)

    @pl.when(block == pl.num_programs(0) - 1)
    def _():
        rows = keep_ref.shape[2]

        def turn(k, carry):
            left, right = totals_ref[k, :, :LANES], totals_ref[k, :, LANES:]
            stack = [left, ahead(left, LANES // 2), right, ahead(right, LANES // 2)]
            lags = jnp.concatenate(stack, axis=0).T
            turned[...] = lags[: LANES // 2]
            for slot in range(parts):
                piece = lax.bitwise_xor(me_ref[0], slot)
                target = send_ref if slot & 1 else keep_ref
                target[slot >> 1, k] = turned[pl.ds(pl.multiple_of(piece * rows, 8), rows), :]
            return carry

        lax.fori_loop(0, templates, turn, 0)


def correlate(arrived, filters, sources, axis):
    blocks, half, window = arrived.shape
    templates = filters.shape[0]
    taps = filters.shape[2]
    pairs = templates * 2
    lags = window - taps
    parts = lax.axis_size(axis)
    cols = lags // SHIFTS
    assert cols == 2 * LANES and LANES == 4 * SHIFTS
    used = window // LANES
    depth = -(-(taps + SHIFTS) // LANES) * LANES
    lanes = arrived.reshape(blocks, half, used, LANES)
    wide = filters.astype(jnp.float32)
    gain = 1.0 / (taps * jnp.sqrt(jnp.mean(wide * wide, axis=2) + EPSILON))
    padded = jnp.pad(wide.reshape(pairs, half, taps), ((0, 0), (0, 0), (0, depth - taps)))

    named = sources.reshape(pairs)
    ids = jnp.arange(pairs, dtype=jnp.int32)
    ahead = (named[None, :] < named[:, None]) | (
        (named[None, :] == named[:, None]) & (ids[None, :] < ids[:, None])
    )
    place = jnp.sum(ahead.astype(jnp.int32), axis=1)
    spots = jnp.arange(pairs + GROUP, dtype=jnp.int32)
    order = jnp.sum(jnp.where(place[None, :] == spots[:, None], ids[None, :], 0), axis=1)
    edges = jnp.arange(blocks + 1, dtype=jnp.int32)
    start = jnp.sum((named[None, :] < edges[:, None]).astype(jnp.int32), axis=1)

    me = lax.axis_index(axis).astype(jnp.int32).reshape(1)
    dims = (templates, half, taps, used, depth, parts)
    smem = pl.BlockSpec(memory_space=pltpu.SMEM)
    piece = (parts // 2, templates, lags // LANES // parts, LANES)
    piece_spec = pl.BlockSpec(piece, lambda b: (0, 0, 0, 0))
    return pl.pallas_call(
        functools.partial(correlate_kernel, dims),
        grid=(blocks,),
        out_shape=[jax.ShapeDtypeStruct(piece, jnp.float32)] * 2,
        in_specs=[
            smem,
            smem,
            smem,
            smem,
            pl.BlockSpec((1, half, used, LANES), lambda b: (b, 0, 0, 0)),
            pl.BlockSpec((pairs, half, depth), lambda b: (0, 0, 0)),
        ],
        out_specs=[piece_spec, piece_spec],
        scratch_shapes=[
            pltpu.VMEM((templates + 1, SHIFTS, cols), jnp.float32),
            pltpu.VMEM((LANES, LANES), jnp.float32),
            pltpu.VMEM((half, depth, cols), jnp.bfloat16),
            pltpu.VMEM((half, GROUP * SHIFTS, depth), jnp.bfloat16),
            pltpu.VMEM((half, SHIFTS, cols), jnp.float32),
            pltpu.VMEM((LANES // 2, LANES), jnp.float32),
        ],
        compiler_params=pltpu.CompilerParams(vmem_limit_bytes=40 * 1024 * 1024),
        name="correlate",
    )(me, start, order, gain.reshape(-1), lanes, padded)


def swapped(x, axis, bit):
    return lax.ppermute(x, axis, [(i, i ^ bit) for i in range(lax.axis_size(axis))])


def per_device(waveform, templates, block_of, trace_of):
    own_index = lax.axis_index("st")
    station_count = lax.axis_size("st")
    own_templates = templates.shape[0]
    group_chans = templates.shape[1]
    half_chans = group_chans // 2
    window = waveform.shape[2]
    sources = block_of[0].reshape(station_count, own_templates, 2)
    own_sources = lax.dynamic_index_in_dim(sources, own_index, 0, keepdims=False)
    wanted = lax.dynamic_index_in_dim(trace_of[0], own_index, 1, keepdims=False)
    source_rows = waveform[wanted.reshape(-1) // 3, wanted.reshape(-1) % 3]
    arrived = lax.all_to_all(
        source_rows.reshape(station_count, half_chans, window),
        "st",
        split_axis=0,
        concat_axis=0,
        tiled=True,
    )
    keep, send = correlate(arrived, templates, own_sources, "ch")
    bit = 1
    while True:
        keep = keep + swapped(send, "ch", bit)
        if keep.shape[0] == 1:
            break
        halves = keep.reshape(keep.shape[0] // 2, 2, *keep.shape[1:])
        keep, send = halves[:, 0], halves[:, 1]
        bit *= 2
    return keep.reshape(own_templates, -1)


def solution(mesh):
    in_specs = (
        P("st", None, None),
        P("st", "ch", None),
        P("ch", None, None),
        P("ch", None, None, None),
    )
    out_specs = P("st", "ch")
    return jax.shard_map(
        per_device, mesh=mesh, in_specs=in_specs, out_specs=out_specs, check_vma=False
    )
```

time: 128 us -> 74.5 us (0.58)
  waiting for transfers between devices: 56.9 us -> 24.2 us
  local copies, waits for them, and re-layouts: 23.8 us -> 8.97 us
  between operations: 13.5 us -> 0.13 us
  Pallas kernels: 24.1 us -> 28.5 us
  starting transfers between devices: 7.29 us -> 8.98 us
  other arithmetic: 1.7 us -> 3.03 us
    reduce_scatter x1 -> x0, waiting for transfers between devices: 43.3 us -> none  [per_device(): lax.psum_scatter(partial_value, 'ch', scatter_dimension=1, tiled=True)]
    ppermute x0 -> x2, waiting for transfers between devices: none -> 12.6 us  [swapped(): lax.ppermute(x, axis, [(i, i ^ bit) for i in range(lax.axis_size(axis))])]
    reshape x4 -> x2, local copies, waits for them, and re-layouts: 8.03 us -> 2.43 us  [the longest x1 1.48 us: correlate(): lanes = arrived.reshape(blocks, half, used, LANES)]
    transpose x2 -> x0, local copies, waits for them, and re-layouts: 4.65 us -> none  [per_device(): partial_value = sums.transpose(0, 2, 1).reshape(own_templates, -1)]
    pallas_call x1, Pallas kernels: 24.1 us -> 28.5 us  [correlate(): pl.pallas_call(functools.partial(correlate_kernel, dims), grid=(blocks,),...]
    unnamed x6 -> x9, local copies, waits for them, and re-layouts: 4.39 us -> 1.06 us
    reduce_scatter x1 -> x0, local copies, waits for them, and re-layouts: 2.34 us -> none  [per_device(): lax.psum_scatter(partial_value, 'ch', scatter_dimension=1, tiled=True)]
    all_to_all x1, waiting for transfers between devices: 13.6 us -> 11.6 us  [per_device(): lax.all_to_all(source_rows.reshape(station_count, half_chans, window), 's...]
  transfers between devices with their start and end apart: 2 -> 3, of which waited for: 2 -> 3; matrix products, arithmetic and copies ran while one was open for 1% -> 5% of each run, Pallas kernels for 0% -> 0%
where the time goes in v1:
time: 74.5 us; the launch traced here: 73.9 us
  Pallas kernels  28.5 us (38%)
  waiting for transfers between devices  24.2 us (32%)
  starting transfers between devices  8.98 us (12%)
  local copies, waits for them, and re-layouts  8.97 us (12%)
  other arithmetic  3.03 us (4%)
    pallas_call x1, Pallas kernels, correlate(): pl.pallas_call(functools.partial(correlate_kernel, dims), grid=(blocks,),...  28.5 us
    ppermute x2, waiting for transfers between devices, swapped(): lax.ppermute(x, axis, [(i, i ^ bit) for i in range(lax.axis_size(axis))])  12.6 us
    all_to_all x1, waiting for transfers between devices, per_device(): lax.all_to_all(source_rows.reshape(station_count, half_chans, window), 's...  11.6 us
    all_to_all x1, starting transfers between devices, per_device(): lax.all_to_all(source_rows.reshape(station_count, half_chans, window), 's...  7.25 us
    gather x1, local copies, waits for them, and re-layouts, per_device(): source_rows = waveform[wanted.reshape(-1) // 3, wanted.reshape(-1) % 3]  2.21 us
    ppermute x2, starting transfers between devices, swapped(): lax.ppermute(x, axis, [(i, i ^ bit) for i in range(lax.axis_size(axis))])  1.73 us
  transfers between devices with their start and end apart: 3, of which 3 were waited for; matrix products, arithmetic and copies ran while one was open for 5% of the time, Pallas kernels for 0%

profile of v1, /device:TPU:0, one launch (start us, length us, event | category | flops | bytes accessed | tf_op | source)
XLA Modules:
  0.0 73.9 jit_solution(9564379020399722604)
XLA Ops:
  0.0 1.1 %fusion.4 = pred[8,4]{1,0:T(8,128)(4,1)S(1)} fusion(s32[1,8,8,4]{2,3,1,0:T(4,128)} %param.7, s32[]{:T(128)S(6)} %select_n.56), kind=kLoop, calls=%fused_computation.16 | loop fusion | flops 64 | bytes 164 | tf_op jit(solution)/shard_map/jit(floor_divide)/ne | solution.py:204
  1.1 1.1 %divide_reduce_fusion = (s32[8,4]{1,0:T(8,128)S(1)}, s32[8,4]{1,0:T(8,128)S(1)}) fusion(s32[1,8,8,4]{2,3,1,0:T(4,128)} %param.7, s32[]{:T(128)S(6)} %select_n.56), kind=kLoop, calls=%fused_computation.15 | loop fusion | flops 64 | bytes 388 | tf_op jit(solution)/shard_map/jit(floor_divide)/div | solution.py:204
  2.3 0.1 ne.52
  2.6 2.2 %gather_fusion = bf16[32,8704]{1,0:T(8,128)(2,1)S(1)} fusion(bf16[32,3,8704]{2,0,1:T(8,128)(2,1)S(1)} %copy-done, s32[32]{0:T(128)S(1)} %fusion.10), kind=kCustom, calls=%fused_computation | custom fusion | bytes 1114368 | tf_op jit(solution)/shard_map/gather | solution.py:204
  4.8 0.9 %reshape.122 = bf16[8,4,8704]{2,1,0:T(4,128)(2,1)} reshape(bf16[32,8704]{1,0:T(8,128)(2,1)S(1)} %gather_fusion) | data formatting | bytes 1114112 | tf_op jit(solution)/shard_map/reshape | solution.py:206
  5.8 7.3 %all-to-all-start = ((bf16[8,4,8704]{2,1,0:T(4,128)(2,1)}), bf16[8,4,8704]{2,1,0:T(4,128)(2,1)}, u32[]{:S(2)}, u32[]{:S(2)}) async-start(bf16[8,4,8704]{2,1,0:T(4,128)(2,1)} %reshape.122), calls=%async_computation | async-start | bytes 1114112 | tf_op jit(solution)/shard_map/all_to_all | solution.py:205
  13.1 0.1 copy.25
  13.2 0.1 lt.74
  13.4 1.2 %reshape.124 = f32[104,4,512]{2,1,0:T(4,128)} reshape(bf16[52,8,512]{2,1,0:T(8,128)(2,1)S(1)} %copy-done.1) | data formatting | bytes 1277952 | tf_op jit(solution)/shard_map/reshape | solution.py:146
  14.5 0.2 multiply_reduce_fusion
  14.8 0.1 copy.21
  14.9 0.1 reshape.128.gain_ref
  15.0 1.3 %pad.4.filters_ref = f32[104,4,640]{2,1,0:T(4,128)S(1)} pad(f32[104,4,512]{2,1,0:T(4,128)} %reshape.124, f32[]{:T(128)} %constant.47.clone.1), padding=0_0x0_0x0_128 | pad | bytes 1916932 | tf_op jit(solution)/shard_map/jit(_pad)/pad | solution.py:146
  16.3 0.1 convert_reduce_fusion.1.start_ref
  16.4 0.2 convert_reduce_fusion
  16.6 0.1 select_reduce_fusion.order_ref
  16.7 11.6 %all-to-all-done = bf16[8,4,8704]{2,1,0:T(4,128)(2,1)} async-done(((bf16[8,4,8704]{2,1,0:T(4,128)(2,1)}), bf16[8,4,8704]{2,1,0:T(4,128)(2,1)}, u32[]{:S(2)}, u32[]{:S(2)}) %all-to-all-start) | async-done | bytes 557088 | tf_op jit(solution)/shard_map/all_to_all | solution.py:205
  28.3 1.5 %reshape.135.lanes_ref = bf16[8,4,68,128]{3,2,1,0:T(8,128)(2,1)S(1)} reshape(bf16[8,4,8704]{2,1,0:T(4,128)(2,1)} %all-to-all-done) | data formatting | bytes 1114112 | tf_op jit(solution)/shard_map/reshape | solution.py:143
  29.8 28.5 %correlate.1 = (f32[2,52,16,128]{3,2,1,0:T(8,128)S(1)}, f32[2,52,16,128]{3,2,1,0:T(8,128)S(1)}) custom-call(s32[1]{0:T(128)} %bitcast.me_ref, s32[9]{0:T(128)S(1)} %convert_reduce_fusion.1.start_ref, s32[108]{0:T(128)S(1)} %select_reduce_fusion.order_ref, f32[416]{0:T(512)S(1)} %reshape.128.gain_ref, bf16[8,4,68,128]{3,2,1,0:T(8,128)(2,1)S(1)} %reshape.135.lanes_ref, ...), custom_call_target="tpu_custom_call" | custom-call | tf_op jit(solution)/shard_map/correlate/pallas_call | solution.py:164
  58.4 2.4 %collective-permute-done = f32[2,52,16,128]{3,2,1,0:T(8,128)S(1)} collective-permute-done((f32[2,52,16,128]{3,2,1,0:T(8,128)S(1)}, f32[2,52,16,128]{3,2,1,0:T(8,128)S(1)}, u32[]{:S(2)}, u32[]{:S(2)}) %collective-permute-start) | collective-permute-done | bytes 852000 | tf_op jit(solution)/shard_map/ppermute | solution.py:191
  60.8 0.1 add_bitcast_fusion
  60.9 1.7 %collective-permute-start.1 = (f32[1,52,16,128]{3,2,1,0:T(8,128)S(1)}, f32[1,52,16,128]{3,2,1,0:T(8,128)S(1)}, u32[]{:S(2)}, u32[]{:S(2)}) collective-permute-start(f32[1,52,16,128]{3,2,1,0:T(8,128)S(1)} %slice_bitcast_fusion), channel_id=1, source_target_pairs={{0,2},{1,3},{2,0},{3,1},{4,6},{5,7},{6,4},{7,5},{8,10},{9,11},{10,... | collective-permute-start | bytes 1277960 | tf_op jit(solution)/shard_map/ppermute | solution.py:191
  62.6 10.3 %collective-permute-done.1 = f32[1,52,16,128]{3,2,1,0:T(8,128)S(1)} collective-permute-done((f32[1,52,16,128]{3,2,1,0:T(8,128)S(1)}, f32[1,52,16,128]{3,2,1,0:T(8,128)S(1)}, u32[]{:S(2)}, u32[]{:S(2)}) %collective-permute-start.1) | collective-permute-done | bytes 426016 | tf_op jit(solution)/shard_map/ppermute | solution.py:191
  72.9 0.9 %copy.26 = f32[7,8,16,128]{3,1,2,0:T(8,128)} copy(f32[7,8,16,128]{3,2,1,0:T(8,128)S(1)} %bitcast.20) | data formatting | bytes 917504
  (17 shorter events, 0.6 us)
Async XLA Ops:
  0.0 2.6 %copy-start = (bf16[32,3,8704]{2,0,1:T(8,128)(2,1)S(1)}, bf16[32,3,8704]{2,0,1:T(8,128)(2,1)}, u32[]{:S(2)}) copy-start(bf16[32,3,8704]{2,0,1:T(8,128)(2,1)} %param.4) | copy-start | bytes 5013508
  4.8 8.2 %copy-start.2 = (s32[1,416,2]{1,2,0:T(2,128)S(1)}, s32[1,416,2]{1,2,0:T(2,128)}, u32[]{:S(2)}) copy-start(s32[1,416,2]{1,2,0:T(2,128)} %param.6) | copy-start | bytes 9988
  4.8 8.5 %copy-start.1 = (bf16[52,8,512]{2,1,0:T(8,128)(2,1)S(1)}, bf16[52,8,512]{2,1,0:T(8,128)(2,1)}, u32[]{:S(2)}) copy-start(bf16[52,8,512]{2,1,0:T(8,128)(2,1)} %param.5) | copy-start | bytes 1277956
  5.8 22.5 %all-to-all-start = ((bf16[8,4,8704]{2,1,0:T(4,128)(2,1)}), bf16[8,4,8704]{2,1,0:T(4,128)(2,1)}, u32[]{:S(2)}, u32[]{:S(2)}) async-start(bf16[8,4,8704]{2,1,0:T(4,128)(2,1)} %reshape.122), calls=%async_computation | async-start | bytes 1114112 | tf_op jit(solution)/shard_map/all_to_all | solution.py:205
  58.3 2.4 %collective-permute-start = (f32[2,52,16,128]{3,2,1,0:T(8,128)S(1)}, f32[2,52,16,128]{3,2,1,0:T(8,128)S(1)}, u32[]{:S(2)}, u32[]{:S(2)}) collective-permute-start(f32[2,52,16,128]{3,2,1,0:T(8,128)S(1)} %get-tuple-element.8), channel_id=1, source_target_pairs={{0,1},{1,0},{2,3},{3,2},{4,5},{5,4},{6,7},{7,6},{8,9},{9,8},{10,11... | collective-permute-start | bytes 2555912 | tf_op jit(solution)/shard_map/ppermute | solution.py:191
  60.9 11.9 %collective-permute-start.1 = (f32[1,52,16,128]{3,2,1,0:T(8,128)S(1)}, f32[1,52,16,128]{3,2,1,0:T(8,128)S(1)}, u32[]{:S(2)}, u32[]{:S(2)}) collective-permute-start(f32[1,52,16,128]{3,2,1,0:T(8,128)S(1)} %slice_bitcast_fusion), channel_id=1, source_target_pairs={{0,2},{1,3},{2,0},{3,1},{4,6},{5,7},{6,4},{7,5},{8,10},{9,11},{10,... | collective-permute-start | bytes 1277960 | tf_op jit(solution)/shard_map/ppermute | solution.py:191

commit v2 on v1

v2 whole, which is shorter than its diff:
```python
import functools
import math

import jax
import jax.numpy as jnp
from jax import lax
from jax.experimental import pallas as pl
from jax.experimental.pallas import tpu as pltpu
from jax.sharding import PartitionSpec as P

EPSILON = 1e-05
SHIFTS = 32
LANES = 128
GROUP = 4


def skew_kernel(dims, owner_ref, order_ref, filters_ref, out_ref):
    half, taps, depth, blocks = dims
    chunk = pl.program_id(0)

    @pl.when(owner_ref[chunk] < blocks)
    def _():
        for g in range(GROUP):
            pair = jnp.maximum(order_ref[chunk * GROUP + g], 0)
            rows = filters_ref[lax.shift_right_logical(pair, 1)].astype(jnp.float32)
            rows = jnp.where(lax.bitwise_and(pair, 1) == 1, rows[half:], rows[:half])
            blank = jnp.zeros((SHIFTS, depth - taps), jnp.float32)
            for c in range(half):
                spread = jnp.broadcast_to(rows[c : c + 1], (SHIFTS, taps))
                spread = jnp.concatenate([spread, blank], axis=1)
                spread = pltpu.roll(spread, 0, 1, stride=1, stride_axis=0)
                out_ref[0, c, g * SHIFTS : (g + 1) * SHIFTS, :] = spread.astype(jnp.bfloat16)


def correlate_kernel(
    dims,
    owner_ref,
    order_ref,
    me_ref,
    gain_ref,
    lanes_ref,
    skewed_ref,
    keep_ref,
    send_ref,
    totals_ref,
    padded,
    hankel,
    scale,
    turned,
):
    templates, half, taps, used, parts, blocks = dims
    chunk = pl.program_id(0)
    owner = owner_ref[chunk]
    earlier = owner_ref[jnp.maximum(chunk - 1, 0)]
    fresh = (owner < blocks) & ((chunk == 0) | (owner != earlier))

    @pl.when(chunk == 0)
    def _():
        totals_ref[...] = jnp.zeros_like(totals_ref)
        hankel[...] = jnp.zeros_like(hankel)
        padded[...] = jnp.zeros_like(padded)

    row = lax.broadcasted_iota(jnp.int32, (LANES, LANES), 0)
    low = lax.broadcasted_iota(jnp.int32, (SHIFTS, LANES), 1) < LANES // 2
    whole = taps // LANES
    splits = LANES // SHIFTS

    def ahead(x, by):
        by = (LANES - by) % LANES
        return x if by == 0 else pltpu.roll(x, by, 1)

    def strip(x, m):
        at = (m % splits) * SHIFTS
        return x[at : at + SHIFTS]

    def joined(x, m):
        left = ahead(strip(x, m), m // splits)
        right = ahead(strip(x, m + 1), (m + 1) // splits - LANES // 2)
        return jnp.where(low, left, right)

    @pl.when(fresh)
    def _():
        for c in range(half):
            padded[:used, :] = lanes_ref[0, c].astype(jnp.float32)
            lanes = padded[...].T
            steps = taps // SHIFTS + 1
            for m in range(steps + 2):
                pair = joined(lanes, m).astype(jnp.bfloat16)
                if m < steps:
                    hankel[c, m * SHIFTS : (m + 1) * SHIFTS, :LANES] = pair
                if m >= 2:
                    hankel[c, (m - 2) * SHIFTS : (m - 1) * SHIFTS, LANES:] = pair
            squares = lanes * lanes
            prefix, suffix = squares, squares
            step = 1
            while step < LANES:
                prefix = prefix + jnp.where(row >= step, pltpu.roll(prefix, step, 0), 0.0)
                suffix = suffix + jnp.where(
                    row < LANES - step, pltpu.roll(suffix, LANES - step, 0), 0.0
                )
                step *= 2
            before = jnp.where(row >= 1, pltpu.roll(prefix, 1, 0), 0.0)
            total = jnp.sum(squares, axis=0, keepdims=True)
            middle = jnp.zeros_like(total)
            for by in range(1, whole):
                middle = middle + ahead(total, by)
            energy = suffix + middle + ahead(before, whole)
            root = lax.rsqrt(energy / taps + EPSILON)
            scale[c, :, :LANES] = joined(root, 0)
            scale[c, :, LANES:] = joined(root, 2)

    @pl.when(owner < blocks)
    def _():
        codes = [order_ref[chunk * GROUP + g] for g in range(GROUP)]
        totals = [None] * GROUP
        for c in range(half):
            raw = jnp.dot(skewed_ref[0, c], hankel[c], preferred_element_type=jnp.float32)
            for g in range(GROUP):
                gain = gain_ref[jnp.maximum(codes[g], 0) * half + c]
                term = raw[g * SHIFTS : (g + 1) * SHIFTS] * (scale[c] * gain)
                totals[g] = term if c == 0 else totals[g] + term
        for g in range(GROUP):
            place = jnp.where(codes[g] >= 0, lax.shift_right_arithmetic(codes[g], 1), templates)
            totals_ref[place] += totals[g]

    @pl.when(chunk == pl.num_programs(0) - 1)
    def _():
        rows = keep_ref.shape[2]

        def turn(k, carry):
            left, right = totals_ref[k, :, :LANES], totals_ref[k, :, LANES:]
            stack = [left, ahead(left, LANES // 2), right, ahead(right, LANES // 2)]
            lags = jnp.concatenate(stack, axis=0).T
            turned[...] = lags[: LANES // 2]
            for slot in range(parts):
                piece = lax.bitwise_xor(me_ref[0], slot)
                target = send_ref if slot & 1 else keep_ref
                target[slot >> 1, k] = turned[pl.ds(pl.multiple_of(piece * rows, 8), rows), :]
            return carry

        lax.fori_loop(0, templates, turn, 0)


def correlate(arrived, filters, sources, axis):
    blocks, half, window = arrived.shape
    templates = filters.shape[0]
    taps = filters.shape[2]
    pairs = templates * 2
    lags = window - taps
    parts = lax.axis_size(axis)
    cols = lags // SHIFTS
    assert cols == 2 * LANES and LANES == 4 * SHIFTS
    used = window // LANES
    depth = -(-(taps + SHIFTS) // LANES) * LANES
    lanes = arrived.reshape(blocks, half, used, LANES)
    wide = filters.astype(jnp.float32)
    gain = 1.0 / (taps * jnp.sqrt(jnp.mean(wide * wide, axis=2) + EPSILON))

    named = sources.reshape(pairs)
    ids = jnp.arange(pairs, dtype=jnp.int32)
    edges = jnp.arange(blocks, dtype=jnp.int32)
    counts = jnp.sum((named[None, :] == edges[:, None]).astype(jnp.int32), axis=1)
    chunks = (counts + (GROUP - 1)) >> (GROUP.bit_length() - 1)
    ends = jnp.sum(jnp.where(edges[None, :] <= edges[:, None], chunks[None, :], 0), axis=1)
    begin = jnp.sum(jnp.where(edges[None, :] < named[:, None], chunks[None, :], 0), axis=1)
    same = (named[None, :] == named[:, None]) & (ids[None, :] < ids[:, None])
    place = begin * GROUP + jnp.sum(same.astype(jnp.int32), axis=1)
    steps = (pairs + blocks * (GROUP - 1)) // GROUP
    spots = jnp.arange(steps * GROUP, dtype=jnp.int32)
    order = jnp.sum(jnp.where(place[None, :] == spots[:, None], ids[None, :] + 1, 0), axis=1) - 1
    numbers = jnp.arange(steps, dtype=jnp.int32)
    owner = jnp.sum((ends[None, :] <= numbers[:, None]).astype(jnp.int32), axis=1)
    me = lax.axis_index(axis).astype(jnp.int32).reshape(1)
    smem = pl.BlockSpec(memory_space=pltpu.SMEM)
    skew_shape = (1, half, GROUP * SHIFTS, depth)
    skewed = pl.pallas_call(
        functools.partial(skew_kernel, (half, taps, depth, blocks)),
        grid_spec=pltpu.PrefetchScalarGridSpec(
            num_scalar_prefetch=2,
            grid=(steps,),
            in_specs=[pl.BlockSpec(filters.shape, lambda i, *_: (0, 0, 0))],
            out_specs=pl.BlockSpec(skew_shape, lambda i, *_: (i, 0, 0, 0)),
        ),
        out_shape=jax.ShapeDtypeStruct((steps,) + skew_shape[1:], jnp.bfloat16),
        compiler_params=pltpu.CompilerParams(vmem_limit_bytes=32 * 1024 * 1024),
        cost_estimate=pl.CostEstimate(
            flops=steps * math.prod(skew_shape) * 16,
            bytes_accessed=steps * math.prod(skew_shape) * 2,
            transcendentals=0,
        ),
        name="skew",
    )(owner, order, filters)

    dims = (templates, half, taps, used, parts, blocks)
    piece = (parts // 2, templates, lags // LANES // parts, LANES)
    piece_spec = pl.BlockSpec(piece, lambda i, *_: (0, 0, 0, 0))

    def lanes_at(i, owners, *_):
        return jnp.minimum(owners[i], blocks - 1), 0, 0, 0

    return pl.pallas_call(
        functools.partial(correlate_kernel, dims),
        grid_spec=pltpu.PrefetchScalarGridSpec(
            num_scalar_prefetch=2,
            grid=(steps,),
            in_specs=[
                smem,
                smem,
                pl.BlockSpec((1, half, used, LANES), lanes_at),
                pl.BlockSpec(skew_shape, lambda i, *_: (i, 0, 0, 0)),
            ],
            out_specs=[piece_spec, piece_spec],
            scratch_shapes=[
                pltpu.VMEM((templates + 1, SHIFTS, cols), jnp.float32),
                pltpu.VMEM((LANES, LANES), jnp.float32),
                pltpu.VMEM((half, depth, cols), jnp.bfloat16),
                pltpu.VMEM((half, SHIFTS, cols), jnp.float32),
                pltpu.VMEM((LANES // 2, LANES), jnp.float32),
            ],
        ),
        out_shape=[jax.ShapeDtypeStruct(piece, jnp.float32)] * 2,
        compiler_params=pltpu.CompilerParams(vmem_limit_bytes=32 * 1024 * 1024),
        name="correlate",
    )(owner, order, me, gain.reshape(-1), lanes, skewed)


def swapped(x, axis, bit):
    return lax.ppermute(x, axis, [(i, i ^ bit) for i in range(lax.axis_size(axis))])


def per_device(waveform, templates, block_of, trace_of):
    own_index = lax.axis_index("st")
    station_count = lax.axis_size("st")
    own_templates = templates.shape[0]
    group_chans = templates.shape[1]
    half_chans = group_chans // 2
    window = waveform.shape[2]
    sources = block_of[0].reshape(station_count, own_templates, 2)
    own_sources = lax.dynamic_index_in_dim(sources, own_index, 0, keepdims=False)
    wanted = lax.dynamic_index_in_dim(trace_of[0], own_index, 1, keepdims=False)
    wanted = wanted.reshape(-1)
    station = (wanted * 43691) >> 17
    source_rows = waveform[station, wanted - 3 * station]
    arrived = lax.all_to_all(
        source_rows.reshape(station_count, half_chans, window),
        "st",
        split_axis=0,
        concat_axis=0,
        tiled=True,
    )
    keep, send = correlate(arrived, templates, own_sources, "ch")
    bit = 1
    while True:
        keep = keep + swapped(send, "ch", bit)
        if keep.shape[0] == 1:
            break
        halves = keep.reshape(keep.shape[0] // 2, 2, *keep.shape[1:])
        keep, send = halves[:, 0], halves[:, 1]
        bit *= 2
    return keep.reshape(own_templates, -1)


def solution(mesh):
    in_specs = (
        P("st", None, None),
        P("st", "ch", None),
        P("ch", None, None),
        P("ch", None, None, None),
    )
    out_specs = P("st", "ch")
    return jax.shard_map(
        per_device, mesh=mesh, in_specs=in_specs, out_specs=out_specs, check_vma=False
    )
```

time: 74.5 us -> 82.7 us (1.11)
  Pallas kernels: 28.5 us -> 46.3 us
  waiting for transfers between devices: 24.2 us -> 13 us
  local copies, waits for them, and re-layouts: 8.97 us -> 13.3 us
  other arithmetic: 3.03 us -> 1.06 us
    pallas_call x1 -> x2, Pallas kernels: 28.5 us -> 46.3 us  [the longest x1 39.1 us: correlate(): pl.pallas_call(functools.partial(correlate_kernel, dims), grid_spec=pltpu...]
    all_to_all x1, waiting for transfers between devices: 11.6 us -> 0.01 us  [per_device(): lax.all_to_all(source_rows.reshape(station_count, half_chans, window), 's...]
    unnamed x9 -> x11, local copies, waits for them, and re-layouts: 1.06 us -> 8.26 us
    pad x1 -> x0, local copies, waits for them, and re-layouts: 1.33 us -> none  [correlate(): jnp.pad(wide.reshape(pairs, half, taps), ((0, 0), (0, 0), (0, depth - tap...]
    reshape x1, local copies, waits for them, and re-layouts: 1.48 us -> 0.21 us  [correlate(): lanes = arrived.reshape(blocks, half, used, LANES)]
    div x1 -> x0, other arithmetic: 1.14 us -> none  [per_device(): source_rows = waveform[wanted.reshape(-1) // 3, wanted.reshape(-1) % 3]]
    ne x1 -> x0, other arithmetic: 1.13 us -> none  [per_device(): source_rows = waveform[wanted.reshape(-1) // 3, wanted.reshape(-1) % 3]]
    dynamic_slice x0 -> x1, local copies, waits for them, and re-layouts: none -> 1.12 us  [per_device(): wanted = lax.dynamic_index_in_dim(trace_of[0], own_index, 1, keepdims=False)]
  transfers between devices with their start and end apart: 3 -> 3, of which waited for: 3 -> 2; matrix products, arithmetic and copies ran while one was open for 5% -> 2% of each run, Pallas kernels for 0% -> 9%
where the time goes in v2:
time: 82.7 us; the launch traced here: 82.4 us
  Pallas kernels  46.3 us (56%)
  local copies, waits for them, and re-layouts  13.3 us (16%)
  waiting for transfers between devices  13 us (16%)
  starting transfers between devices  8.63 us (10%)
  other arithmetic  1.06 us (1%)
    pallas_call x1, Pallas kernels, correlate(): pl.pallas_call(functools.partial(correlate_kernel, dims), grid_spec=pltpu...  39.1 us
    ppermute x2, waiting for transfers between devices, swapped(): lax.ppermute(x, axis, [(i, i ^ bit) for i in range(lax.axis_size(axis))])  13 us
    unnamed x11, local copies, waits for them, and re-layouts  8.26 us
    all_to_all x1, starting transfers between devices, per_device(): lax.all_to_all(source_rows.reshape(station_count, half_chans, window), 's...  7.25 us
    pallas_call x1, Pallas kernels, correlate(): pl.pallas_call(functools.partial(skew_kernel, (half, taps, depth, blocks)...  7.19 us
    gather x1, local copies, waits for them, and re-layouts, per_device(): source_rows = waveform[station, wanted - 3 * station]  2.21 us
  transfers between devices with their start and end apart: 3, of which 2 were waited for; matrix products, arithmetic and copies ran while one was open for 2% of the time, Pallas kernels for 9%

profile of v2, /device:TPU:0, one launch (start us, length us, event | category | flops | bytes accessed | tf_op | source)
XLA Modules:
  0.0 82.4 jit_solution(8751567902216026221)
XLA Ops:
  0.0 1.1 %dynamic-slice_reduce_fusion = s32[8,4]{1,0:T(8,128)S(1)} fusion(s32[1,8,8,4]{2,3,1,0:T(4,128)} %param.7, s32[]{:T(128)S(6)} %select_n.38), kind=kLoop, calls=%fused_computation.12 | loop fusion | bytes 260 | tf_op jit(solution)/shard_map/jit(dynamic_index_in_dim)/dynamic_slice | solution.py:240
  1.2 0.2 copy-done
  1.5 2.2 %gather_fusion = bf16[32,8704]{1,0:T(8,128)(2,1)S(1)} fusion(bf16[32,3,8704]{2,0,1:T(8,128)(2,1)S(1)} %copy-done, s32[32]{0:T(128)S(1)} %fusion.8), kind=kCustom, calls=%fused_computation | custom fusion | bytes 1114368 | tf_op jit(solution)/shard_map/gather | solution.py:243
  3.7 0.9 %reshape.99 = bf16[8,4,8704]{2,1,0:T(4,128)(2,1)} reshape(bf16[32,8704]{1,0:T(8,128)(2,1)S(1)} %gather_fusion) | data formatting | bytes 1114112 | tf_op jit(solution)/shard_map/reshape | solution.py:245
  4.6 7.3 %all-to-all-start = ((bf16[8,4,8704]{2,1,0:T(4,128)(2,1)}), bf16[8,4,8704]{2,1,0:T(4,128)(2,1)S(1)}, u32[]{:S(2)}, u32[]{:S(2)}) async-start(bf16[8,4,8704]{2,1,0:T(4,128)(2,1)} %reshape.99), calls=%async_computation | async-start | bytes 1114112 | tf_op jit(solution)/shard_map/all_to_all | solution.py:244
  12.0 0.1 copy.25
  12.1 0.1 eq.20
  12.2 0.1 convert_reduce_fusion.2
  12.3 0.2 multiply_reduce_fusion
  12.6 0.1 select_reduce_fusion.2
  12.7 0.1 copy.21
  12.8 0.1 reshape.104.gain_ref
  12.9 0.1 convert_reduce_fusion.1.owner_ref
  13.1 0.2 convert_reduce_fusion
  13.3 0.1 select_reduce_fusion
  13.4 7.2 %skew.1.skewed_ref = bf16[32,4,128,640]{3,2,1,0:T(8,128)(2,1)S(1)} custom-call(s32[32]{0:T(128)S(1)} %convert_reduce_fusion.1.owner_ref, s32[128]{0:T(128)S(1)} %broadcast_add_fusion.order_ref, bf16[52,8,512]{2,1,0:T(8,128)(2,1)S(1)} %copy-done.2), custom_call_target="tpu_custom_call" | custom-call | flops 167772160 | bytes 20971520 | tf_op jit(solution)/shard_map/skew/pallas_call | solution.py:176
  20.6 7.0 %copy-done.1 = bf16[32,4,128,640]{3,2,1,0:T(8,128)(2,1)} copy-done((bf16[32,4,128,640]{3,2,1,0:T(8,128)(2,1)}, bf16[32,4,128,640]{3,2,1,0:T(8,128)(2,1)S(1)}, u32[]{:S(2)}) %copy-start.1) | copy-done | bytes 20971544
  27.6 0.2 reshape.111.lanes_ref
  27.8 39.1 %correlate.1 = (f32[2,52,16,128]{3,2,1,0:T(8,128)S(1)}, f32[2,52,16,128]{3,2,1,0:T(8,128)S(1)}) custom-call(s32[32]{0:T(128)S(1)} %convert_reduce_fusion.1.owner_ref, s32[128]{0:T(128)S(1)} %broadcast_add_fusion.order_ref, s32[1]{0:T(128)} %bitcast.me_ref, f32[416]{0:T(512)S(1)} %reshape.104.gain_ref, bf16[8,4,68,128]{3,2,1,0:T(8,128)(2,1)S(1)} %reshape.111.lanes_ref, ...), custom_call_target="tpu_custom_call" | custom-call | tf_op jit(solution)/shard_map/correlate/pallas_call | solution.py:201
  67.0 2.4 %collective-permute-done = f32[2,52,16,128]{3,2,1,0:T(8,128)S(1)} collective-permute-done((f32[2,52,16,128]{3,2,1,0:T(8,128)S(1)}, f32[2,52,16,128]{3,2,1,0:T(8,128)S(1)}, u32[]{:S(2)}, u32[]{:S(2)}) %collective-permute-start) | collective-permute-done | bytes 852000 | tf_op jit(solution)/shard_map/ppermute | solution.py:228
  69.4 0.1 add_bitcast_fusion
  69.5 1.3 %collective-permute-start.1 = (f32[1,52,16,128]{3,2,1,0:T(8,128)S(1)}, f32[1,52,16,128]{3,2,1,0:T(8,128)S(1)}, u32[]{:S(2)}, u32[]{:S(2)}) collective-permute-start(f32[1,52,16,128]{3,2,1,0:T(8,128)S(1)} %slice_bitcast_fusion), channel_id=1, source_target_pairs={{0,2},{1,3},{2,0},{3,1},{4,6},{5,7},{6,4},{7,5},{8,10},{9,11},{10,... | collective-permute-start | bytes 1277960 | tf_op jit(solution)/shard_map/ppermute | solution.py:228
  70.8 10.6 %collective-permute-done.1 = f32[1,52,16,128]{3,2,1,0:T(8,128)S(1)} collective-permute-done((f32[1,52,16,128]{3,2,1,0:T(8,128)S(1)}, f32[1,52,16,128]{3,2,1,0:T(8,128)S(1)}, u32[]{:S(2)}, u32[]{:S(2)}) %collective-permute-start.1) | collective-permute-done | bytes 426016 | tf_op jit(solution)/shard_map/ppermute | solution.py:228
  81.5 0.9 %copy.26 = f32[7,8,16,128]{3,1,2,0:T(8,128)} copy(f32[7,8,16,128]{3,2,1,0:T(8,128)S(1)} %bitcast.20) | data formatting | bytes 917504
  (21 shorter events, 0.6 us)
Async XLA Ops:
  0.0 1.5 %copy-start = (bf16[32,3,8704]{2,0,1:T(8,128)(2,1)S(1)}, bf16[32,3,8704]{2,0,1:T(8,128)(2,1)}, u32[]{:S(2)}) copy-start(bf16[32,3,8704]{2,0,1:T(8,128)(2,1)} %param.4) | copy-start | bytes 5013508
  3.7 8.2 %copy-start.3 = (s32[1,416,2]{1,2,0:T(2,128)S(1)}, s32[1,416,2]{1,2,0:T(2,128)}, u32[]{:S(2)}) copy-start(s32[1,416,2]{1,2,0:T(2,128)} %param.6) | copy-start | bytes 9988
  3.7 8.7 %copy-start.2 = (bf16[52,8,512]{2,1,0:T(8,128)(2,1)S(1)}, bf16[52,8,512]{2,1,0:T(8,128)(2,1)}, u32[]{:S(2)}) copy-start(bf16[52,8,512]{2,1,0:T(8,128)(2,1)} %filters_ref.1) | copy-start | bytes 1277956
  4.6 22.9 %all-to-all-start = ((bf16[8,4,8704]{2,1,0:T(4,128)(2,1)}), bf16[8,4,8704]{2,1,0:T(4,128)(2,1)S(1)}, u32[]{:S(2)}, u32[]{:S(2)}) async-start(bf16[8,4,8704]{2,1,0:T(4,128)(2,1)} %reshape.99), calls=%async_computation | async-start | bytes 1114112 | tf_op jit(solution)/shard_map/all_to_all | solution.py:244
  20.6 7.0 %copy-start.1 = (bf16[32,4,128,640]{3,2,1,0:T(8,128)(2,1)}, bf16[32,4,128,640]{3,2,1,0:T(8,128)(2,1)S(1)}, u32[]{:S(2)}) copy-start(bf16[32,4,128,640]{3,2,1,0:T(8,128)(2,1)S(1)} %skew.1.skewed_ref) | copy-start | bytes 62914564
  66.9 2.4 %collective-permute-start = (f32[2,52,16,128]{3,2,1,0:T(8,128)S(1)}, f32[2,52,16,128]{3,2,1,0:T(8,128)S(1)}, u32[]{:S(2)}, u32[]{:S(2)}) collective-permute-start(f32[2,52,16,128]{3,2,1,0:T(8,128)S(1)} %get-tuple-element.8), channel_id=1, source_target_pairs={{0,1},{1,0},{2,3},{3,2},{4,5},{5,4},{6,7},{7,6},{8,9},{9,8},{10,11... | collective-permute-start | bytes 2555912 | tf_op jit(solution)/shard_map/ppermute | solution.py:228
  69.5 11.9 %collective-permute-start.1 = (f32[1,52,16,128]{3,2,1,0:T(8,128)S(1)}, f32[1,52,16,128]{3,2,1,0:T(8,128)S(1)}, u32[]{:S(2)}, u32[]{:S(2)}) collective-permute-start(f32[1,52,16,128]{3,2,1,0:T(8,128)S(1)} %slice_bitcast_fusion), channel_id=1, source_target_pairs={{0,2},{1,3},{2,0},{3,1},{4,6},{5,7},{6,4},{7,5},{8,10},{9,11},{10,... | collective-permute-start | bytes 1277960 | tf_op jit(solution)/shard_map/ppermute | solution.py:228

commit v3 on v1

--- a/solution.py
+++ b/solution.py
@@ -19,6 +19,7 @@
     start_ref,
     order_ref,
     gain_ref,
+    steps_ref,
     lanes_ref,
     filters_ref,
     keep_ref,
@@ -39,7 +40,6 @@
         hankel[...] = jnp.zeros_like(hankel)
         padded[...] = jnp.zeros_like(padded)
 
-    row = lax.broadcasted_iota(jnp.int32, (LANES, LANES), 0)
     low = lax.broadcasted_iota(jnp.int32, (SHIFTS, LANES), 1) < LANES // 2
     whole = taps // LANES
     splits = LANES // SHIFTS
@@ -68,16 +68,16 @@
             if m >= 2:
                 hankel[c, (m - 2) * SHIFTS : (m - 1) * SHIFTS, LANES:] = pair
         squares = lanes * lanes
-        prefix, suffix = squares, squares
-        step = 1
-        while step < LANES:
-            prefix = prefix + jnp.where(row >= step, pltpu.roll(prefix, step, 0), 0.0)
-            suffix = suffix + jnp.where(
-                row < LANES - step, pltpu.roll(suffix, LANES - step, 0), 0.0
-            )
-            step *= 2
-        before = jnp.where(row >= 1, pltpu.roll(prefix, 1, 0), 0.0)
-        total = jnp.sum(squares, axis=0, keepdims=True)
+        high = squares.astype(jnp.bfloat16)
+        rest = (squares - high.astype(jnp.float32)).astype(jnp.bfloat16)
+        sums = jnp.dot(
+            steps_ref[...],
+            jnp.concatenate([high, rest], axis=1),
+            preferred_element_type=jnp.float32,
+        )
+        sums = sums[:, :LANES] + sums[:, LANES:]
+        before, suffix = sums[:LANES], sums[LANES:]
+        total = suffix[0:1]
         middle = jnp.zeros_like(total)
         for by in range(1, whole):
             middle = middle + ahead(total, by)
@@ -156,6 +156,9 @@
     edges = jnp.arange(blocks + 1, dtype=jnp.int32)
     start = jnp.sum((named[None, :] < edges[:, None]).astype(jnp.int32), axis=1)
 
+    spots = jnp.arange(LANES)
+    earlier = spots[None, :] < spots[:, None]
+    steps = jnp.concatenate([earlier, ~earlier], axis=0).astype(jnp.bfloat16)
     me = lax.axis_index(axis).astype(jnp.int32).reshape(1)
     dims = (templates, half, taps, used, depth, parts)
     smem = pl.BlockSpec(memory_space=pltpu.SMEM)
@@ -170,6 +173,7 @@
             smem,
             smem,
             smem,
+            pl.BlockSpec((2 * LANES, LANES), lambda b: (0, 0)),
             pl.BlockSpec((1, half, used, LANES), lambda b: (b, 0, 0, 0)),
             pl.BlockSpec((pairs, half, depth), lambda b: (0, 0, 0)),
         ],
@@ -184,7 +188,7 @@
         ],
         compiler_params=pltpu.CompilerParams(vmem_limit_bytes=40 * 1024 * 1024),
         name="correlate",
-    )(me, start, order, gain.reshape(-1), lanes, padded)
+    )(me, start, order, gain.reshape(-1), steps, lanes, padded)
 
 
 def swapped(x, axis, bit):
@@ -201,7 +205,9 @@
     sources = block_of[0].reshape(station_count, own_templates, 2)
     own_sources = lax.dynamic_index_in_dim(sources, own_index, 0, keepdims=False)
     wanted = lax.dynamic_index_in_dim(trace_of[0], own_index, 1, keepdims=False)
-    source_rows = waveform[wanted.reshape(-1) // 3, wanted.reshape(-1) % 3]
+    wanted = wanted.reshape(-1)
+    station = (wanted * 43691) >> 17
+    source_rows = waveform[station, wanted - 3 * station]
     arrived = lax.all_to_all(
         source_rows.reshape(station_count, half_chans, window),
         "st",

time: 74.5 us -> 73.9 us (level)
  other arithmetic: 3.03 us -> 0.78 us
  local copies, waits for them, and re-layouts: 8.97 us -> 10.1 us
  Pallas kernels: 28.5 us -> 29.4 us
    div x1 -> x0, other arithmetic: 1.14 us -> none  [per_device(): source_rows = waveform[wanted.reshape(-1) // 3, wanted.reshape(-1) % 3]]
    ne x1 -> x0, other arithmetic: 1.13 us -> none  [per_device(): source_rows = waveform[wanted.reshape(-1) // 3, wanted.reshape(-1) % 3]]
    dynamic_slice x0 -> x1, local copies, waits for them, and re-layouts: none -> 1.12 us  [per_device(): wanted = lax.dynamic_index_in_dim(trace_of[0], own_index, 1, keepdims=False)]
    pallas_call x1, Pallas kernels: 28.5 us -> 29.4 us  [correlate(): pl.pallas_call(functools.partial(correlate_kernel, dims), grid=(blocks,),...]
where the time goes in v3:
time: 73.9 us; the launch traced here: 73.7 us
  Pallas kernels  29.4 us (40%)
  waiting for transfers between devices  24.2 us (33%)
  local copies, waits for them, and re-layouts  10.1 us (14%)
  starting transfers between devices  8.96 us (12%)
  other arithmetic  0.78 us (1%)
    pallas_call x1, Pallas kernels, correlate(): pl.pallas_call(functools.partial(correlate_kernel, dims), grid=(blocks,),...  29.4 us
    ppermute x2, waiting for transfers between devices, swapped(): lax.ppermute(x, axis, [(i, i ^ bit) for i in range(lax.axis_size(axis))])  12.7 us
    all_to_all x1, waiting for transfers between devices, per_device(): lax.all_to_all(source_rows.reshape(station_count, half_chans, window), 's...  11.6 us
    all_to_all x1, starting transfers between devices, per_device(): lax.all_to_all(source_rows.reshape(station_count, half_chans, window), 's...  7.25 us
    gather x1, local copies, waits for them, and re-layouts, per_device(): source_rows = waveform[station, wanted - 3 * station]  2.21 us
    ppermute x2, starting transfers between devices, swapped(): lax.ppermute(x, axis, [(i, i ^ bit) for i in range(lax.axis_size(axis))])  1.7 us
    reshape x1, local copies, waits for them, and re-layouts, correlate(): lanes = arrived.reshape(blocks, half, used, LANES)  1.48 us
  transfers between devices with their start and end apart: 3, of which 3 were waited for; matrix products, arithmetic and copies ran while one was open for 5% of the time, Pallas kernels for 0%

profile of v3, /device:TPU:0, one launch (start us, length us, event | category | flops | bytes accessed | tf_op | source)
XLA Modules:
  0.0 73.7 jit_solution(264953193967490373)
XLA Ops:
  0.0 1.1 %dynamic-slice_reduce_fusion = s32[8,4]{1,0:T(8,128)S(1)} fusion(s32[1,8,8,4]{2,3,1,0:T(4,128)} %param.7, s32[]{:T(128)S(6)} %select_n.30), kind=kLoop, calls=%fused_computation.16 | loop fusion | bytes 260 | tf_op jit(solution)/shard_map/jit(dynamic_index_in_dim)/dynamic_slice | solution.py:207
  1.1 0.1 reshape.86
  1.2 0.2 copy-done
  1.5 2.2 %gather_fusion = bf16[32,8704]{1,0:T(8,128)(2,1)S(1)} fusion(bf16[32,3,8704]{2,0,1:T(8,128)(2,1)S(1)} %copy-done, s32[32]{0:T(128)S(1)} %fusion.10), kind=kCustom, calls=%fused_computation | custom fusion | bytes 1114368 | tf_op jit(solution)/shard_map/gather | solution.py:210
  3.7 0.9 %reshape.87 = bf16[8,4,8704]{2,1,0:T(4,128)(2,1)} reshape(bf16[32,8704]{1,0:T(8,128)(2,1)S(1)} %gather_fusion) | data formatting | bytes 1114112 | tf_op jit(solution)/shard_map/reshape | solution.py:212
  4.6 7.3 %all-to-all-start = ((bf16[8,4,8704]{2,1,0:T(4,128)(2,1)}), bf16[8,4,8704]{2,1,0:T(4,128)(2,1)}, u32[]{:S(2)}, u32[]{:S(2)}) async-start(bf16[8,4,8704]{2,1,0:T(4,128)(2,1)} %reshape.87), calls=%async_computation | async-start | bytes 1114112 | tf_op jit(solution)/shard_map/all_to_all | solution.py:211
  12.0 0.1 copy.25
  12.1 0.1 lt.87
  12.2 1.2 %reshape.89 = f32[104,4,512]{2,1,0:T(4,128)} reshape(bf16[52,8,512]{2,1,0:T(8,128)(2,1)S(1)} %copy-done.1) | data formatting | bytes 1277952 | tf_op jit(solution)/shard_map/reshape | solution.py:146
  13.4 0.2 multiply_reduce_fusion
  13.7 0.1 copy.21
  13.8 0.1 reshape.93.gain_ref
  13.9 1.3 %pad.4.filters_ref = f32[104,4,640]{2,1,0:T(4,128)S(1)} pad(f32[104,4,512]{2,1,0:T(4,128)} %reshape.89, f32[]{:T(128)} %constant.13.clone.1), padding=0_0x0_0x0_128 | pad | bytes 1916932 | tf_op jit(solution)/shard_map/jit(_pad)/pad | solution.py:146
  15.2 0.1 convert_reduce_fusion.1.start_ref
  15.4 0.2 convert_reduce_fusion
  15.5 0.1 select_reduce_fusion.order_ref
  15.6 11.6 %all-to-all-done = bf16[8,4,8704]{2,1,0:T(4,128)(2,1)} async-done(((bf16[8,4,8704]{2,1,0:T(4,128)(2,1)}), bf16[8,4,8704]{2,1,0:T(4,128)(2,1)}, u32[]{:S(2)}, u32[]{:S(2)}) %all-to-all-start) | async-done | bytes 557088 | tf_op jit(solution)/shard_map/all_to_all | solution.py:211
  27.2 1.5 %reshape.100.lanes_ref = bf16[8,4,68,128]{3,2,1,0:T(8,128)(2,1)S(1)} reshape(bf16[8,4,8704]{2,1,0:T(4,128)(2,1)} %all-to-all-done) | data formatting | bytes 1114112 | tf_op jit(solution)/shard_map/reshape | solution.py:143
  28.7 29.4 %correlate.1 = (f32[2,52,16,128]{3,2,1,0:T(8,128)S(1)}, f32[2,52,16,128]{3,2,1,0:T(8,128)S(1)}) custom-call(s32[1]{0:T(128)} %bitcast.me_ref, s32[9]{0:T(128)S(1)} %convert_reduce_fusion.1.start_ref, s32[108]{0:T(128)S(1)} %select_reduce_fusion.order_ref, f32[416]{0:T(512)S(1)} %reshape.93.gain_ref, bf16[256,128]{1,0:T(8,128)(2,1)S(1)} %add_convert_fusion.steps_ref, ...), custom_call_target="tpu_custom_call" | custom-call | tf_op jit(solution)/shard_map/correlate/pallas_call | solution.py:167
  58.2 2.4 %collective-permute-done = f32[2,52,16,128]{3,2,1,0:T(8,128)S(1)} collective-permute-done((f32[2,52,16,128]{3,2,1,0:T(8,128)S(1)}, f32[2,52,16,128]{3,2,1,0:T(8,128)S(1)}, u32[]{:S(2)}, u32[]{:S(2)}) %collective-permute-start) | collective-permute-done | bytes 852000 | tf_op jit(solution)/shard_map/ppermute | solution.py:195
  60.6 0.1 add_bitcast_fusion
  60.7 1.6 %collective-permute-start.1 = (f32[1,52,16,128]{3,2,1,0:T(8,128)S(1)}, f32[1,52,16,128]{3,2,1,0:T(8,128)S(1)}, u32[]{:S(2)}, u32[]{:S(2)}) collective-permute-start(f32[1,52,16,128]{3,2,1,0:T(8,128)S(1)} %slice_bitcast_fusion), channel_id=1, source_target_pairs={{0,2},{1,3},{2,0},{3,1},{4,6},{5,7},{6,4},{7,5},{8,10},{9,11},{10,... | collective-permute-start | bytes 1277960 | tf_op jit(solution)/shard_map/ppermute | solution.py:195
  62.4 10.3 %collective-permute-done.1 = f32[1,52,16,128]{3,2,1,0:T(8,128)S(1)} collective-permute-done((f32[1,52,16,128]{3,2,1,0:T(8,128)S(1)}, f32[1,52,16,128]{3,2,1,0:T(8,128)S(1)}, u32[]{:S(2)}, u32[]{:S(2)}) %collective-permute-start.1) | collective-permute-done | bytes 426016 | tf_op jit(solution)/shard_map/ppermute | solution.py:195
  72.7 0.9 %copy.26 = f32[7,8,16,128]{3,1,2,0:T(8,128)} copy(f32[7,8,16,128]{3,2,1,0:T(8,128)S(1)} %bitcast.20) | data formatting | bytes 917504
  (16 shorter events, 0.4 us)
Async XLA Ops:
  0.0 1.5 %copy-start = (bf16[32,3,8704]{2,0,1:T(8,128)(2,1)S(1)}, bf16[32,3,8704]{2,0,1:T(8,128)(2,1)}, u32[]{:S(2)}) copy-start(bf16[32,3,8704]{2,0,1:T(8,128)(2,1)} %param.4) | copy-start | bytes 5013508
  3.7 8.2 %copy-start.2 = (s32[1,416,2]{1,2,0:T(2,128)S(1)}, s32[1,416,2]{1,2,0:T(2,128)}, u32[]{:S(2)}) copy-start(s32[1,416,2]{1,2,0:T(2,128)} %param.6) | copy-start | bytes 9988
  3.7 8.5 %copy-start.1 = (bf16[52,8,512]{2,1,0:T(8,128)(2,1)S(1)}, bf16[52,8,512]{2,1,0:T(8,128)(2,1)}, u32[]{:S(2)}) copy-start(bf16[52,8,512]{2,1,0:T(8,128)(2,1)} %param.5) | copy-start | bytes 1277956
  4.6 22.5 %all-to-all-start = ((bf16[8,4,8704]{2,1,0:T(4,128)(2,1)}), bf16[8,4,8704]{2,1,0:T(4,128)(2,1)}, u32[]{:S(2)}, u32[]{:S(2)}) async-start(bf16[8,4,8704]{2,1,0:T(4,128)(2,1)} %reshape.87), calls=%async_computation | async-start | bytes 1114112 | tf_op jit(solution)/shard_map/all_to_all | solution.py:211
  58.1 2.4 %collective-permute-start = (f32[2,52,16,128]{3,2,1,0:T(8,128)S(1)}, f32[2,52,16,128]{3,2,1,0:T(8,128)S(1)}, u32[]{:S(2)}, u32[]{:S(2)}) collective-permute-start(f32[2,52,16,128]{3,2,1,0:T(8,128)S(1)} %get-tuple-element.8), channel_id=1, source_target_pairs={{0,1},{1,0},{2,3},{3,2},{4,5},{5,4},{6,7},{7,6},{8,9},{9,8},{10,11... | collective-permute-start | bytes 2555912 | tf_op jit(solution)/shard_map/ppermute | solution.py:195
  60.7 11.9 %collective-permute-start.1 = (f32[1,52,16,128]{3,2,1,0:T(8,128)S(1)}, f32[1,52,16,128]{3,2,1,0:T(8,128)S(1)}, u32[]{:S(2)}, u32[]{:S(2)}) collective-permute-start(f32[1,52,16,128]{3,2,1,0:T(8,128)S(1)} %slice_bitcast_fusion), channel_id=1, source_target_pairs={{0,2},{1,3},{2,0},{3,1},{4,6},{5,7},{6,4},{7,5},{8,10},{9,11},{10,... | collective-permute-start | bytes 1277960 | tf_op jit(solution)/shard_map/ppermute | solution.py:195

commit v4 on v3

--- a/solution.py
+++ b/solution.py
@@ -10,7 +10,7 @@
 EPSILON = 1e-05
 SHIFTS = 32
 LANES = 128
-GROUP = 4
+GROUP = 8
 
 
 def correlate_kernel(

time: 73.9 us -> 73.2 us (level)
  Pallas kernels: 29.4 us -> 28 us
    pallas_call x1, Pallas kernels: 29.4 us -> 28 us  [correlate(): pl.pallas_call(functools.partial(correlate_kernel, dims), grid=(blocks,),...]
where the time goes in v4:
time: 73.2 us; the launch traced here: 72.8 us
  Pallas kernels  28 us (38%)
  waiting for transfers between devices  24 us (33%)
  local copies, waits for them, and re-layouts  10.1 us (14%)
  starting transfers between devices  9.67 us (13%)
  other arithmetic  0.78 us (1%)
    pallas_call x1, Pallas kernels, correlate(): pl.pallas_call(functools.partial(correlate_kernel, dims), grid=(blocks,),...  28 us
    ppermute x2, waiting for transfers between devices, swapped(): lax.ppermute(x, axis, [(i, i ^ bit) for i in range(lax.axis_size(axis))])  12.5 us
    all_to_all x1, waiting for transfers between devices, per_device(): lax.all_to_all(source_rows.reshape(station_count, half_chans, window), 's...  11.6 us
    all_to_all x1, starting transfers between devices, per_device(): lax.all_to_all(source_rows.reshape(station_count, half_chans, window), 's...  7.25 us
    ppermute x2, starting transfers between devices, swapped(): lax.ppermute(x, axis, [(i, i ^ bit) for i in range(lax.axis_size(axis))])  2.41 us
    gather x1, local copies, waits for them, and re-layouts, per_device(): source_rows = waveform[station, wanted - 3 * station]  2.21 us
    reshape x1, local copies, waits for them, and re-layouts, correlate(): lanes = arrived.reshape(blocks, half, used, LANES)  1.48 us
  transfers between devices with their start and end apart: 3, of which 3 were waited for; matrix products, arithmetic and copies ran while one was open for 5% of the time, Pallas kernels for 0%

profile of v4, /device:TPU:0, one launch (start us, length us, event | category | flops | bytes accessed | tf_op | source)
XLA Modules:
  0.0 72.8 jit_solution(7008686693391458893)
XLA Ops:
  0.0 1.1 %dynamic-slice_reduce_fusion = s32[8,4]{1,0:T(8,128)S(1)} fusion(s32[1,8,8,4]{2,3,1,0:T(4,128)} %param.7, s32[]{:T(128)S(6)} %select_n.30), kind=kLoop, calls=%fused_computation.16 | loop fusion | bytes 260 | tf_op jit(solution)/shard_map/jit(dynamic_index_in_dim)/dynamic_slice | solution.py:207
  1.1 0.1 reshape.86
  1.2 0.2 copy-done
  1.5 2.2 %gather_fusion = bf16[32,8704]{1,0:T(8,128)(2,1)S(1)} fusion(bf16[32,3,8704]{2,0,1:T(8,128)(2,1)S(1)} %copy-done, s32[32]{0:T(128)S(1)} %fusion.10), kind=kCustom, calls=%fused_computation | custom fusion | bytes 1114368 | tf_op jit(solution)/shard_map/gather | solution.py:210
  3.7 0.9 %reshape.87 = bf16[8,4,8704]{2,1,0:T(4,128)(2,1)} reshape(bf16[32,8704]{1,0:T(8,128)(2,1)S(1)} %gather_fusion) | data formatting | bytes 1114112 | tf_op jit(solution)/shard_map/reshape | solution.py:212
  4.6 7.3 %all-to-all-start = ((bf16[8,4,8704]{2,1,0:T(4,128)(2,1)}), bf16[8,4,8704]{2,1,0:T(4,128)(2,1)}, u32[]{:S(2)}, u32[]{:S(2)}) async-start(bf16[8,4,8704]{2,1,0:T(4,128)(2,1)} %reshape.87), calls=%async_computation | async-start | bytes 1114112 | tf_op jit(solution)/shard_map/all_to_all | solution.py:211
  12.0 0.1 copy.25
  12.1 0.1 lt.87
  12.2 1.2 %reshape.89 = f32[104,4,512]{2,1,0:T(4,128)} reshape(bf16[52,8,512]{2,1,0:T(8,128)(2,1)S(1)} %copy-done.1) | data formatting | bytes 1277952 | tf_op jit(solution)/shard_map/reshape | solution.py:146
  13.4 0.2 multiply_reduce_fusion
  13.7 0.1 copy.21
  13.8 0.1 reshape.93.gain_ref
  13.9 1.3 %pad.4.filters_ref = f32[104,4,640]{2,1,0:T(4,128)S(1)} pad(f32[104,4,512]{2,1,0:T(4,128)} %reshape.89, f32[]{:T(128)} %constant.13.clone.1), padding=0_0x0_0x0_128 | pad | bytes 1916932 | tf_op jit(solution)/shard_map/jit(_pad)/pad | solution.py:146
  15.2 0.1 convert_reduce_fusion.1.start_ref
  15.4 0.2 convert_reduce_fusion
  15.5 0.1 select_reduce_fusion.order_ref
  15.6 11.6 %all-to-all-done = bf16[8,4,8704]{2,1,0:T(4,128)(2,1)} async-done(((bf16[8,4,8704]{2,1,0:T(4,128)(2,1)}), bf16[8,4,8704]{2,1,0:T(4,128)(2,1)}, u32[]{:S(2)}, u32[]{:S(2)}) %all-to-all-start) | async-done | bytes 557088 | tf_op jit(solution)/shard_map/all_to_all | solution.py:211
  27.2 1.5 %reshape.100.lanes_ref = bf16[8,4,68,128]{3,2,1,0:T(8,128)(2,1)S(1)} reshape(bf16[8,4,8704]{2,1,0:T(4,128)(2,1)} %all-to-all-done) | data formatting | bytes 1114112 | tf_op jit(solution)/shard_map/reshape | solution.py:143
  28.7 28.0 %correlate.1 = (f32[2,52,16,128]{3,2,1,0:T(8,128)S(1)}, f32[2,52,16,128]{3,2,1,0:T(8,128)S(1)}) custom-call(s32[1]{0:T(128)} %bitcast.me_ref, s32[9]{0:T(128)S(1)} %convert_reduce_fusion.1.start_ref, s32[112]{0:T(128)S(1)} %select_reduce_fusion.order_ref, f32[416]{0:T(512)S(1)} %reshape.93.gain_ref, bf16[256,128]{1,0:T(8,128)(2,1)S(1)} %add_convert_fusion.steps_ref, ...), custom_call_target="tpu_custom_call" | custom-call | tf_op jit(solution)/shard_map/correlate/pallas_call | solution.py:167
  56.8 2.4 %collective-permute-done = f32[2,52,16,128]{3,2,1,0:T(8,128)S(1)} collective-permute-done((f32[2,52,16,128]{3,2,1,0:T(8,128)S(1)}, f32[2,52,16,128]{3,2,1,0:T(8,128)S(1)}, u32[]{:S(2)}, u32[]{:S(2)}) %collective-permute-start) | collective-permute-done | bytes 852000 | tf_op jit(solution)/shard_map/ppermute | solution.py:195
  59.2 0.1 add_bitcast_fusion
  59.3 2.3 %collective-permute-start.1 = (f32[1,52,16,128]{3,2,1,0:T(8,128)S(1)}, f32[1,52,16,128]{3,2,1,0:T(8,128)S(1)}, u32[]{:S(2)}, u32[]{:S(2)}) collective-permute-start(f32[1,52,16,128]{3,2,1,0:T(8,128)S(1)} %slice_bitcast_fusion), channel_id=1, source_target_pairs={{0,2},{1,3},{2,0},{3,1},{4,6},{5,7},{6,4},{7,5},{8,10},{9,11},{10,... | collective-permute-start | bytes 1277960 | tf_op jit(solution)/shard_map/ppermute | solution.py:195
  61.7 10.1 %collective-permute-done.1 = f32[1,52,16,128]{3,2,1,0:T(8,128)S(1)} collective-permute-done((f32[1,52,16,128]{3,2,1,0:T(8,128)S(1)}, f32[1,52,16,128]{3,2,1,0:T(8,128)S(1)}, u32[]{:S(2)}, u32[]{:S(2)}) %collective-permute-start.1) | collective-permute-done | bytes 426016 | tf_op jit(solution)/shard_map/ppermute | solution.py:195
  71.9 0.9 %copy.26 = f32[7,8,16,128]{3,1,2,0:T(8,128)} copy(f32[7,8,16,128]{3,2,1,0:T(8,128)S(1)} %bitcast.20) | data formatting | bytes 917504
  (16 shorter events, 0.4 us)
Async XLA Ops:
  0.0 1.5 %copy-start = (bf16[32,3,8704]{2,0,1:T(8,128)(2,1)S(1)}, bf16[32,3,8704]{2,0,1:T(8,128)(2,1)}, u32[]{:S(2)}) copy-start(bf16[32,3,8704]{2,0,1:T(8,128)(2,1)} %param.4) | copy-start | bytes 5013508
  3.7 8.2 %copy-start.2 = (s32[1,416,2]{1,2,0:T(2,128)S(1)}, s32[1,416,2]{1,2,0:T(2,128)}, u32[]{:S(2)}) copy-start(s32[1,416,2]{1,2,0:T(2,128)} %param.6) | copy-start | bytes 9988
  3.7 8.5 %copy-start.1 = (bf16[52,8,512]{2,1,0:T(8,128)(2,1)S(1)}, bf16[52,8,512]{2,1,0:T(8,128)(2,1)}, u32[]{:S(2)}) copy-start(bf16[52,8,512]{2,1,0:T(8,128)(2,1)} %param.5) | copy-start | bytes 1277956
  4.6 22.5 %all-to-all-start = ((bf16[8,4,8704]{2,1,0:T(4,128)(2,1)}), bf16[8,4,8704]{2,1,0:T(4,128)(2,1)}, u32[]{:S(2)}, u32[]{:S(2)}) async-start(bf16[8,4,8704]{2,1,0:T(4,128)(2,1)} %reshape.87), calls=%async_computation | async-start | bytes 1114112 | tf_op jit(solution)/shard_map/all_to_all | solution.py:211
  56.7 2.4 %collective-permute-start = (f32[2,52,16,128]{3,2,1,0:T(8,128)S(1)}, f32[2,52,16,128]{3,2,1,0:T(8,128)S(1)}, u32[]{:S(2)}, u32[]{:S(2)}) collective-permute-start(f32[2,52,16,128]{3,2,1,0:T(8,128)S(1)} %get-tuple-element.8), channel_id=1, source_target_pairs={{0,1},{1,0},{2,3},{3,2},{4,5},{5,4},{6,7},{7,6},{8,9},{9,8},{10,11... | collective-permute-start | bytes 2555912 | tf_op jit(solution)/shard_map/ppermute | solution.py:195
  59.3 12.5 %collective-permute-start.1 = (f32[1,52,16,128]{3,2,1,0:T(8,128)S(1)}, f32[1,52,16,128]{3,2,1,0:T(8,128)S(1)}, u32[]{:S(2)}, u32[]{:S(2)}) collective-permute-start(f32[1,52,16,128]{3,2,1,0:T(8,128)S(1)} %slice_bitcast_fusion), channel_id=1, source_target_pairs={{0,2},{1,3},{2,0},{3,1},{4,6},{5,7},{6,4},{7,5},{8,10},{9,11},{10,... | collective-permute-start | bytes 1277960 | tf_op jit(solution)/shard_map/ppermute | solution.py:195

commit v5 on v4

--- a/solution.py
+++ b/solution.py
@@ -10,7 +10,7 @@
 EPSILON = 1e-05
 SHIFTS = 32
 LANES = 128
-GROUP = 8
+GROUP = 17
 
 
 def correlate_kernel(

time: 73.2 us -> 71.6 us (0.978)
  Pallas kernels: 28 us -> 27.1 us
    pallas_call x1, Pallas kernels: 28 us -> 27.1 us  [correlate(): pl.pallas_call(functools.partial(correlate_kernel, dims), grid=(blocks,),...]
where the time goes in v5:
time: 71.6 us; the launch traced here: 71.3 us
  Pallas kernels  27.1 us (38%)
  waiting for transfers between devices  24.2 us (34%)
  local copies, waits for them, and re-layouts  10.1 us (14%)
  starting transfers between devices  8.97 us (13%)
  other arithmetic  0.78 us (1%)
    pallas_call x1, Pallas kernels, correlate(): pl.pallas_call(functools.partial(correlate_kernel, dims), grid=(blocks,),...  27.1 us
    ppermute x2, waiting for transfers between devices, swapped(): lax.ppermute(x, axis, [(i, i ^ bit) for i in range(lax.axis_size(axis))])  12.6 us
    all_to_all x1, waiting for transfers between devices, per_device(): lax.all_to_all(source_rows.reshape(station_count, half_chans, window), 's...  11.6 us
    all_to_all x1, starting transfers between devices, per_device(): lax.all_to_all(source_rows.reshape(station_count, half_chans, window), 's...  7.25 us
    gather x1, local copies, waits for them, and re-layouts, per_device(): source_rows = waveform[station, wanted - 3 * station]  2.21 us
    ppermute x2, starting transfers between devices, swapped(): lax.ppermute(x, axis, [(i, i ^ bit) for i in range(lax.axis_size(axis))])  1.71 us
    reshape x1, local copies, waits for them, and re-layouts, correlate(): lanes = arrived.reshape(blocks, half, used, LANES)  1.48 us
  transfers between devices with their start and end apart: 3, of which 3 were waited for; matrix products, arithmetic and copies ran while one was open for 5% of the time, Pallas kernels for 0%

profile of v5, /device:TPU:0, one launch (start us, length us, event | category | flops | bytes accessed | tf_op | source)
XLA Modules:
  0.0 71.3 jit_solution(13840571165620403456)
XLA Ops:
  0.0 1.1 %dynamic-slice_reduce_fusion = s32[8,4]{1,0:T(8,128)S(1)} fusion(s32[1,8,8,4]{2,3,1,0:T(4,128)} %param.7, s32[]{:T(128)S(6)} %select_n.30), kind=kLoop, calls=%fused_computation.16 | loop fusion | bytes 260 | tf_op jit(solution)/shard_map/jit(dynamic_index_in_dim)/dynamic_slice | solution.py:207
  1.1 0.1 reshape.86
  1.2 0.2 copy-done
  1.5 2.2 %gather_fusion = bf16[32,8704]{1,0:T(8,128)(2,1)S(1)} fusion(bf16[32,3,8704]{2,0,1:T(8,128)(2,1)S(1)} %copy-done, s32[32]{0:T(128)S(1)} %fusion.10), kind=kCustom, calls=%fused_computation | custom fusion | bytes 1114368 | tf_op jit(solution)/shard_map/gather | solution.py:210
  3.7 0.9 %reshape.87 = bf16[8,4,8704]{2,1,0:T(4,128)(2,1)} reshape(bf16[32,8704]{1,0:T(8,128)(2,1)S(1)} %gather_fusion) | data formatting | bytes 1114112 | tf_op jit(solution)/shard_map/reshape | solution.py:212
  4.6 7.3 %all-to-all-start = ((bf16[8,4,8704]{2,1,0:T(4,128)(2,1)}), bf16[8,4,8704]{2,1,0:T(4,128)(2,1)}, u32[]{:S(2)}, u32[]{:S(2)}) async-start(bf16[8,4,8704]{2,1,0:T(4,128)(2,1)} %reshape.87), calls=%async_computation | async-start | bytes 1114112 | tf_op jit(solution)/shard_map/all_to_all | solution.py:211
  12.0 0.1 copy.25
  12.1 0.1 lt.87
  12.2 1.2 %reshape.89 = f32[104,4,512]{2,1,0:T(4,128)} reshape(bf16[52,8,512]{2,1,0:T(8,128)(2,1)S(1)} %copy-done.1) | data formatting | bytes 1277952 | tf_op jit(solution)/shard_map/reshape | solution.py:146
  13.4 0.2 multiply_reduce_fusion
  13.7 0.1 copy.21
  13.8 0.1 reshape.93.gain_ref
  13.9 1.3 %pad.4.filters_ref = f32[104,4,640]{2,1,0:T(4,128)S(1)} pad(f32[104,4,512]{2,1,0:T(4,128)} %reshape.89, f32[]{:T(128)} %constant.13.clone.1), padding=0_0x0_0x0_128 | pad | bytes 1916932 | tf_op jit(solution)/shard_map/jit(_pad)/pad | solution.py:146
  15.2 0.1 convert_reduce_fusion.1.start_ref
  15.4 0.2 convert_reduce_fusion
  15.5 0.1 select_reduce_fusion.order_ref
  15.6 11.6 %all-to-all-done = bf16[8,4,8704]{2,1,0:T(4,128)(2,1)} async-done(((bf16[8,4,8704]{2,1,0:T(4,128)(2,1)}), bf16[8,4,8704]{2,1,0:T(4,128)(2,1)}, u32[]{:S(2)}, u32[]{:S(2)}) %all-to-all-start) | async-done | bytes 557088 | tf_op jit(solution)/shard_map/all_to_all | solution.py:211
  27.2 1.5 %reshape.100.lanes_ref = bf16[8,4,68,128]{3,2,1,0:T(8,128)(2,1)S(1)} reshape(bf16[8,4,8704]{2,1,0:T(4,128)(2,1)} %all-to-all-done) | data formatting | bytes 1114112 | tf_op jit(solution)/shard_map/reshape | solution.py:143
  28.7 27.1 %correlate.1 = (f32[2,52,16,128]{3,2,1,0:T(8,128)S(1)}, f32[2,52,16,128]{3,2,1,0:T(8,128)S(1)}) custom-call(s32[1]{0:T(128)} %bitcast.me_ref, s32[9]{0:T(128)S(1)} %convert_reduce_fusion.1.start_ref, s32[121]{0:T(128)S(1)} %select_reduce_fusion.order_ref, f32[416]{0:T(512)S(1)} %reshape.93.gain_ref, bf16[256,128]{1,0:T(8,128)(2,1)S(1)} %add_convert_fusion.steps_ref, ...), custom_call_target="tpu_custom_call" | custom-call | tf_op jit(solution)/shard_map/correlate/pallas_call | solution.py:167
  55.8 2.4 %collective-permute-done = f32[2,52,16,128]{3,2,1,0:T(8,128)S(1)} collective-permute-done((f32[2,52,16,128]{3,2,1,0:T(8,128)S(1)}, f32[2,52,16,128]{3,2,1,0:T(8,128)S(1)}, u32[]{:S(2)}, u32[]{:S(2)}) %collective-permute-start) | collective-permute-done | bytes 852000 | tf_op jit(solution)/shard_map/ppermute | solution.py:195
  58.2 0.1 add_bitcast_fusion
  58.4 1.6 %collective-permute-start.1 = (f32[1,52,16,128]{3,2,1,0:T(8,128)S(1)}, f32[1,52,16,128]{3,2,1,0:T(8,128)S(1)}, u32[]{:S(2)}, u32[]{:S(2)}) collective-permute-start(f32[1,52,16,128]{3,2,1,0:T(8,128)S(1)} %slice_bitcast_fusion), channel_id=1, source_target_pairs={{0,2},{1,3},{2,0},{3,1},{4,6},{5,7},{6,4},{7,5},{8,10},{9,11},{10,... | collective-permute-start | bytes 1277960 | tf_op jit(solution)/shard_map/ppermute | solution.py:195
  60.0 10.3 %collective-permute-done.1 = f32[1,52,16,128]{3,2,1,0:T(8,128)S(1)} collective-permute-done((f32[1,52,16,128]{3,2,1,0:T(8,128)S(1)}, f32[1,52,16,128]{3,2,1,0:T(8,128)S(1)}, u32[]{:S(2)}, u32[]{:S(2)}) %collective-permute-start.1) | collective-permute-done | bytes 426016 | tf_op jit(solution)/shard_map/ppermute | solution.py:195
  70.4 0.9 %copy.26 = f32[7,8,16,128]{3,1,2,0:T(8,128)} copy(f32[7,8,16,128]{3,2,1,0:T(8,128)S(1)} %bitcast.20) | data formatting | bytes 917504
  (16 shorter events, 0.4 us)
Async XLA Ops:
  0.0 1.5 %copy-start = (bf16[32,3,8704]{2,0,1:T(8,128)(2,1)S(1)}, bf16[32,3,8704]{2,0,1:T(8,128)(2,1)}, u32[]{:S(2)}) copy-start(bf16[32,3,8704]{2,0,1:T(8,128)(2,1)} %param.4) | copy-start | bytes 5013508
  3.7 8.2 %copy-start.2 = (s32[1,416,2]{1,2,0:T(2,128)S(1)}, s32[1,416,2]{1,2,0:T(2,128)}, u32[]{:S(2)}) copy-start(s32[1,416,2]{1,2,0:T(2,128)} %param.6) | copy-start | bytes 9988
  3.7 8.5 %copy-start.1 = (bf16[52,8,512]{2,1,0:T(8,128)(2,1)S(1)}, bf16[52,8,512]{2,1,0:T(8,128)(2,1)}, u32[]{:S(2)}) copy-start(bf16[52,8,512]{2,1,0:T(8,128)(2,1)} %param.5) | copy-start | bytes 1277956
  4.6 22.5 %all-to-all-start = ((bf16[8,4,8704]{2,1,0:T(4,128)(2,1)}), bf16[8,4,8704]{2,1,0:T(4,128)(2,1)}, u32[]{:S(2)}, u32[]{:S(2)}) async-start(bf16[8,4,8704]{2,1,0:T(4,128)(2,1)} %reshape.87), calls=%async_computation | async-start | bytes 1114112 | tf_op jit(solution)/shard_map/all_to_all | solution.py:211
  55.8 2.4 %collective-permute-start = (f32[2,52,16,128]{3,2,1,0:T(8,128)S(1)}, f32[2,52,16,128]{3,2,1,0:T(8,128)S(1)}, u32[]{:S(2)}, u32[]{:S(2)}) collective-permute-start(f32[2,52,16,128]{3,2,1,0:T(8,128)S(1)} %get-tuple-element.8), channel_id=1, source_target_pairs={{0,1},{1,0},{2,3},{3,2},{4,5},{5,4},{6,7},{7,6},{8,9},{9,8},{10,11... | collective-permute-start | bytes 2555912 | tf_op jit(solution)/shard_map/ppermute | solution.py:195
  58.4 11.9 %collective-permute-start.1 = (f32[1,52,16,128]{3,2,1,0:T(8,128)S(1)}, f32[1,52,16,128]{3,2,1,0:T(8,128)S(1)}, u32[]{:S(2)}, u32[]{:S(2)}) collective-permute-start(f32[1,52,16,128]{3,2,1,0:T(8,128)S(1)} %slice_bitcast_fusion), channel_id=1, source_target_pairs={{0,2},{1,3},{2,0},{3,1},{4,6},{5,7},{6,4},{7,5},{8,10},{9,11},{10,... | collective-permute-start | bytes 1277960 | tf_op jit(solution)/shard_map/ppermute | solution.py:195

commit v6 on v5

--- a/solution.py
+++ b/solution.py
@@ -1,4 +1,5 @@
 import functools
+import math
 
 import jax
 import jax.numpy as jnp
@@ -115,18 +116,23 @@
     def _():
         rows = keep_ref.shape[2]
 
-        def turn(k, carry):
-            left, right = totals_ref[k, :, :LANES], totals_ref[k, :, LANES:]
-            stack = [left, ahead(left, LANES // 2), right, ahead(right, LANES // 2)]
-            lags = jnp.concatenate(stack, axis=0).T
-            turned[...] = lags[: LANES // 2]
+        batch = turned.shape[0]
+
+        def turn(number, carry):
+            for j in range(batch):
+                k = number * batch + j
+                left, right = totals_ref[k, :, :LANES], totals_ref[k, :, LANES:]
+                stack = [left, ahead(left, LANES // 2), right, ahead(right, LANES // 2)]
+                turned[j] = jnp.concatenate(stack, axis=0).T[: LANES // 2]
             for slot in range(parts):
                 piece = lax.bitwise_xor(me_ref[0], slot)
+                at = pl.ds(pl.multiple_of(piece * rows, 8), rows)
                 target = send_ref if slot & 1 else keep_ref
-                target[slot >> 1, k] = turned[pl.ds(pl.multiple_of(piece * rows, 8), rows), :]
+                for j in range(batch):
+                    target[slot >> 1, number * batch + j] = turned[j, at, :]
             return carry
 
-        lax.fori_loop(0, templates, turn, 0)
+        lax.fori_loop(0, templates // batch, turn, 0)
 
 
 def correlate(arrived, filters, sources, axis):
@@ -184,7 +190,7 @@
             pltpu.VMEM((half, depth, cols), jnp.bfloat16),
             pltpu.VMEM((half, GROUP * SHIFTS, depth), jnp.bfloat16),
             pltpu.VMEM((half, SHIFTS, cols), jnp.float32),
-            pltpu.VMEM((LANES // 2, LANES), jnp.float32),
+            pltpu.VMEM((math.gcd(templates, 4), LANES // 2, LANES), jnp.float32),
         ],
         compiler_params=pltpu.CompilerParams(vmem_limit_bytes=40 * 1024 * 1024),
         name="correlate",

time: 71.6 us -> 66.4 us (0.927)
  Pallas kernels: 27.1 us -> 21.9 us
    pallas_call x1, Pallas kernels: 27.1 us -> 21.9 us  [correlate(): pl.pallas_call(functools.partial(correlate_kernel, dims), grid=(blocks,),...]
  transfers between devices with their start and end apart: 3 -> 3, of which waited for: 3 -> 3; matrix products, arithmetic and copies ran while one was open for 5% -> 6% of each run, Pallas kernels for 0% -> 0%
where the time goes in v6:
time: 66.4 us; the launch traced here: 66.1 us
  waiting for transfers between devices  24.2 us (36%)
  Pallas kernels  21.9 us (33%)
  local copies, waits for them, and re-layouts  10.1 us (15%)
  starting transfers between devices  8.93 us (13%)
  other arithmetic  0.78 us (1%)
    pallas_call x1, Pallas kernels, correlate(): pl.pallas_call(functools.partial(correlate_kernel, dims), grid=(blocks,),...  21.9 us
    ppermute x2, waiting for transfers between devices, swapped(): lax.ppermute(x, axis, [(i, i ^ bit) for i in range(lax.axis_size(axis))])  12.7 us
    all_to_all x1, waiting for transfers between devices, per_device(): lax.all_to_all(source_rows.reshape(station_count, half_chans, window), 's...  11.6 us
    all_to_all x1, starting transfers between devices, per_device(): lax.all_to_all(source_rows.reshape(station_count, half_chans, window), 's...  7.25 us
    gather x1, local copies, waits for them, and re-layouts, per_device(): source_rows = waveform[station, wanted - 3 * station]  2.21 us
    ppermute x2, starting transfers between devices, swapped(): lax.ppermute(x, axis, [(i, i ^ bit) for i in range(lax.axis_size(axis))])  1.67 us
    reshape x1, local copies, waits for them, and re-layouts, correlate(): lanes = arrived.reshape(blocks, half, used, LANES)  1.48 us
  transfers between devices with their start and end apart: 3, of which 3 were waited for; matrix products, arithmetic and copies ran while one was open for 6% of the time, Pallas kernels for 0%

profile of v6, /device:TPU:0, one launch (start us, length us, event | category | flops | bytes accessed | tf_op | source)
XLA Modules:
  0.0 66.1 jit_solution(2433634629499463906)
XLA Ops:
  0.0 1.1 %dynamic-slice_reduce_fusion = s32[8,4]{1,0:T(8,128)S(1)} fusion(s32[1,8,8,4]{2,3,1,0:T(4,128)} %param.7, s32[]{:T(128)S(6)} %select_n.30), kind=kLoop, calls=%fused_computation.16 | loop fusion | bytes 260 | tf_op jit(solution)/shard_map/jit(dynamic_index_in_dim)/dynamic_slice | solution.py:213
  1.1 0.1 reshape.86
  1.2 0.2 copy-done
  1.5 2.2 %gather_fusion = bf16[32,8704]{1,0:T(8,128)(2,1)S(1)} fusion(bf16[32,3,8704]{2,0,1:T(8,128)(2,1)S(1)} %copy-done, s32[32]{0:T(128)S(1)} %fusion.10), kind=kCustom, calls=%fused_computation | custom fusion | bytes 1114368 | tf_op jit(solution)/shard_map/gather | solution.py:216
  3.7 0.9 %reshape.87 = bf16[8,4,8704]{2,1,0:T(4,128)(2,1)} reshape(bf16[32,8704]{1,0:T(8,128)(2,1)S(1)} %gather_fusion) | data formatting | bytes 1114112 | tf_op jit(solution)/shard_map/reshape | solution.py:218
  4.6 7.3 %all-to-all-start = ((bf16[8,4,8704]{2,1,0:T(4,128)(2,1)}), bf16[8,4,8704]{2,1,0:T(4,128)(2,1)}, u32[]{:S(2)}, u32[]{:S(2)}) async-start(bf16[8,4,8704]{2,1,0:T(4,128)(2,1)} %reshape.87), calls=%async_computation | async-start | bytes 1114112 | tf_op jit(solution)/shard_map/all_to_all | solution.py:217
  12.0 0.1 copy.25
  12.1 0.1 lt.87
  12.2 1.2 %reshape.89 = f32[104,4,512]{2,1,0:T(4,128)} reshape(bf16[52,8,512]{2,1,0:T(8,128)(2,1)S(1)} %copy-done.1) | data formatting | bytes 1277952 | tf_op jit(solution)/shard_map/reshape | solution.py:152
  13.4 0.2 multiply_reduce_fusion
  13.7 0.1 copy.21
  13.8 0.1 reshape.93.gain_ref
  13.9 1.3 %pad.4.filters_ref = f32[104,4,640]{2,1,0:T(4,128)S(1)} pad(f32[104,4,512]{2,1,0:T(4,128)} %reshape.89, f32[]{:T(128)} %constant.13.clone.1), padding=0_0x0_0x0_128 | pad | bytes 1916932 | tf_op jit(solution)/shard_map/jit(_pad)/pad | solution.py:152
  15.2 0.1 convert_reduce_fusion.1.start_ref
  15.4 0.2 convert_reduce_fusion
  15.5 0.1 select_reduce_fusion.order_ref
  15.6 11.6 %all-to-all-done = bf16[8,4,8704]{2,1,0:T(4,128)(2,1)} async-done(((bf16[8,4,8704]{2,1,0:T(4,128)(2,1)}), bf16[8,4,8704]{2,1,0:T(4,128)(2,1)}, u32[]{:S(2)}, u32[]{:S(2)}) %all-to-all-start) | async-done | bytes 557088 | tf_op jit(solution)/shard_map/all_to_all | solution.py:217
  27.2 1.5 %reshape.100.lanes_ref = bf16[8,4,68,128]{3,2,1,0:T(8,128)(2,1)S(1)} reshape(bf16[8,4,8704]{2,1,0:T(4,128)(2,1)} %all-to-all-done) | data formatting | bytes 1114112 | tf_op jit(solution)/shard_map/reshape | solution.py:149
  28.7 21.9 %correlate.1 = (f32[2,52,16,128]{3,2,1,0:T(8,128)S(1)}, f32[2,52,16,128]{3,2,1,0:T(8,128)S(1)}) custom-call(s32[1]{0:T(128)} %bitcast.me_ref, s32[9]{0:T(128)S(1)} %convert_reduce_fusion.1.start_ref, s32[121]{0:T(128)S(1)} %select_reduce_fusion.order_ref, f32[416]{0:T(512)S(1)} %reshape.93.gain_ref, bf16[256,128]{1,0:T(8,128)(2,1)S(1)} %add_convert_fusion.steps_ref, ...), custom_call_target="tpu_custom_call" | custom-call | tf_op jit(solution)/shard_map/correlate/pallas_call | solution.py:173
  50.7 2.4 %collective-permute-done = f32[2,52,16,128]{3,2,1,0:T(8,128)S(1)} collective-permute-done((f32[2,52,16,128]{3,2,1,0:T(8,128)S(1)}, f32[2,52,16,128]{3,2,1,0:T(8,128)S(1)}, u32[]{:S(2)}, u32[]{:S(2)}) %collective-permute-start) | collective-permute-done | bytes 852000 | tf_op jit(solution)/shard_map/ppermute | solution.py:201
  53.0 0.1 add_bitcast_fusion
  53.2 1.6 %collective-permute-start.1 = (f32[1,52,16,128]{3,2,1,0:T(8,128)S(1)}, f32[1,52,16,128]{3,2,1,0:T(8,128)S(1)}, u32[]{:S(2)}, u32[]{:S(2)}) collective-permute-start(f32[1,52,16,128]{3,2,1,0:T(8,128)S(1)} %slice_bitcast_fusion), channel_id=1, source_target_pairs={{0,2},{1,3},{2,0},{3,1},{4,6},{5,7},{6,4},{7,5},{8,10},{9,11},{10,... | collective-permute-start | bytes 1277960 | tf_op jit(solution)/shard_map/ppermute | solution.py:201
  54.8 10.3 %collective-permute-done.1 = f32[1,52,16,128]{3,2,1,0:T(8,128)S(1)} collective-permute-done((f32[1,52,16,128]{3,2,1,0:T(8,128)S(1)}, f32[1,52,16,128]{3,2,1,0:T(8,128)S(1)}, u32[]{:S(2)}, u32[]{:S(2)}) %collective-permute-start.1) | collective-permute-done | bytes 426016 | tf_op jit(solution)/shard_map/ppermute | solution.py:201
  65.2 0.9 %copy.26 = f32[7,8,16,128]{3,1,2,0:T(8,128)} copy(f32[7,8,16,128]{3,2,1,0:T(8,128)S(1)} %bitcast.20) | data formatting | bytes 917504
  (16 shorter events, 0.4 us)
Async XLA Ops:
  0.0 1.5 %copy-start = (bf16[32,3,8704]{2,0,1:T(8,128)(2,1)S(1)}, bf16[32,3,8704]{2,0,1:T(8,128)(2,1)}, u32[]{:S(2)}) copy-start(bf16[32,3,8704]{2,0,1:T(8,128)(2,1)} %param.4) | copy-start | bytes 5013508
  3.7 8.2 %copy-start.2 = (s32[1,416,2]{1,2,0:T(2,128)S(1)}, s32[1,416,2]{1,2,0:T(2,128)}, u32[]{:S(2)}) copy-start(s32[1,416,2]{1,2,0:T(2,128)} %param.6) | copy-start | bytes 9988
  3.7 8.5 %copy-start.1 = (bf16[52,8,512]{2,1,0:T(8,128)(2,1)S(1)}, bf16[52,8,512]{2,1,0:T(8,128)(2,1)}, u32[]{:S(2)}) copy-start(bf16[52,8,512]{2,1,0:T(8,128)(2,1)} %param.5) | copy-start | bytes 1277956
  4.6 22.5 %all-to-all-start = ((bf16[8,4,8704]{2,1,0:T(4,128)(2,1)}), bf16[8,4,8704]{2,1,0:T(4,128)(2,1)}, u32[]{:S(2)}, u32[]{:S(2)}) async-start(bf16[8,4,8704]{2,1,0:T(4,128)(2,1)} %reshape.87), calls=%async_computation | async-start | bytes 1114112 | tf_op jit(solution)/shard_map/all_to_all | solution.py:217
  50.6 2.4 %collective-permute-start = (f32[2,52,16,128]{3,2,1,0:T(8,128)S(1)}, f32[2,52,16,128]{3,2,1,0:T(8,128)S(1)}, u32[]{:S(2)}, u32[]{:S(2)}) collective-permute-start(f32[2,52,16,128]{3,2,1,0:T(8,128)S(1)} %get-tuple-element.8), channel_id=1, source_target_pairs={{0,1},{1,0},{2,3},{3,2},{4,5},{5,4},{6,7},{7,6},{8,9},{9,8},{10,11... | collective-permute-start | bytes 2555912 | tf_op jit(solution)/shard_map/ppermute | solution.py:201
  53.2 11.9 %collective-permute-start.1 = (f32[1,52,16,128]{3,2,1,0:T(8,128)S(1)}, f32[1,52,16,128]{3,2,1,0:T(8,128)S(1)}, u32[]{:S(2)}, u32[]{:S(2)}) collective-permute-start(f32[1,52,16,128]{3,2,1,0:T(8,128)S(1)} %slice_bitcast_fusion), channel_id=1, source_target_pairs={{0,2},{1,3},{2,0},{3,1},{4,6},{5,7},{6,4},{7,5},{8,10},{9,11},{10,... | collective-permute-start | bytes 1277960 | tf_op jit(solution)/shard_map/ppermute | solution.py:201

commit v7 on v6

--- a/solution.py
+++ b/solution.py
@@ -190,7 +190,7 @@
             pltpu.VMEM((half, depth, cols), jnp.bfloat16),
             pltpu.VMEM((half, GROUP * SHIFTS, depth), jnp.bfloat16),
             pltpu.VMEM((half, SHIFTS, cols), jnp.float32),
-            pltpu.VMEM((math.gcd(templates, 4), LANES // 2, LANES), jnp.float32),
+            pltpu.VMEM((math.gcd(templates, 13), LANES // 2, LANES), jnp.float32),
         ],
         compiler_params=pltpu.CompilerParams(vmem_limit_bytes=40 * 1024 * 1024),
         name="correlate",

time: 66.4 us -> 65.6 us (0.988)
  Pallas kernels: 21.9 us -> 21.1 us
    pallas_call x1, Pallas kernels: 21.9 us -> 21.1 us  [correlate(): pl.pallas_call(functools.partial(correlate_kernel, dims), grid=(blocks,),...]
where the time goes in v7:
time: 65.6 us; the launch traced here: 65.3 us
  waiting for transfers between devices  24.2 us (37%)
  Pallas kernels  21.1 us (32%)
  local copies, waits for them, and re-layouts  10.1 us (15%)
  starting transfers between devices  8.92 us (14%)
  other arithmetic  0.78 us (1%)
    pallas_call x1, Pallas kernels, correlate(): pl.pallas_call(functools.partial(correlate_kernel, dims), grid=(blocks,),...  21.1 us
    ppermute x2, waiting for transfers between devices, swapped(): lax.ppermute(x, axis, [(i, i ^ bit) for i in range(lax.axis_size(axis))])  12.7 us
    all_to_all x1, waiting for transfers between devices, per_device(): lax.all_to_all(source_rows.reshape(station_count, half_chans, window), 's...  11.6 us
    all_to_all x1, starting transfers between devices, per_device(): lax.all_to_all(source_rows.reshape(station_count, half_chans, window), 's...  7.25 us
    gather x1, local copies, waits for them, and re-layouts, per_device(): source_rows = waveform[station, wanted - 3 * station]  2.21 us
    ppermute x2, starting transfers between devices, swapped(): lax.ppermute(x, axis, [(i, i ^ bit) for i in range(lax.axis_size(axis))])  1.67 us
    reshape x1, local copies, waits for them, and re-layouts, correlate(): lanes = arrived.reshape(blocks, half, used, LANES)  1.48 us
    pad x1, local copies, waits for them, and re-layouts, correlate(): jnp.pad(wide.reshape(pairs, half, taps), ((0, 0), (0, 0), (0, depth - tap...  1.33 us
  transfers between devices with their start and end apart: 3, of which 3 were waited for; matrix products, arithmetic and copies ran while one was open for 6% of the time, Pallas kernels for 0%

profile of v7, /device:TPU:0, one launch (start us, length us, event | category | flops | bytes accessed | tf_op | source)
XLA Modules:
  0.0 65.3 jit_solution(4682482397738081655)
XLA Ops:
  0.0 1.1 %dynamic-slice_reduce_fusion = s32[8,4]{1,0:T(8,128)S(1)} fusion(s32[1,8,8,4]{2,3,1,0:T(4,128)} %param.7, s32[]{:T(128)S(6)} %select_n.30), kind=kLoop, calls=%fused_computation.16 | loop fusion | bytes 260 | tf_op jit(solution)/shard_map/jit(dynamic_index_in_dim)/dynamic_slice | solution.py:213
  1.1 0.1 reshape.86
  1.2 0.2 copy-done
  1.5 2.2 %gather_fusion = bf16[32,8704]{1,0:T(8,128)(2,1)S(1)} fusion(bf16[32,3,8704]{2,0,1:T(8,128)(2,1)S(1)} %copy-done, s32[32]{0:T(128)S(1)} %fusion.10), kind=kCustom, calls=%fused_computation | custom fusion | bytes 1114368 | tf_op jit(solution)/shard_map/gather | solution.py:216
  3.7 0.9 %reshape.87 = bf16[8,4,8704]{2,1,0:T(4,128)(2,1)} reshape(bf16[32,8704]{1,0:T(8,128)(2,1)S(1)} %gather_fusion) | data formatting | bytes 1114112 | tf_op jit(solution)/shard_map/reshape | solution.py:218
  4.6 7.3 %all-to-all-start = ((bf16[8,4,8704]{2,1,0:T(4,128)(2,1)}), bf16[8,4,8704]{2,1,0:T(4,128)(2,1)}, u32[]{:S(2)}, u32[]{:S(2)}) async-start(bf16[8,4,8704]{2,1,0:T(4,128)(2,1)} %reshape.87), calls=%async_computation | async-start | bytes 1114112 | tf_op jit(solution)/shard_map/all_to_all | solution.py:217
  12.0 0.1 copy.25
  12.1 0.1 lt.87
  12.2 1.2 %reshape.89 = f32[104,4,512]{2,1,0:T(4,128)} reshape(bf16[52,8,512]{2,1,0:T(8,128)(2,1)S(1)} %copy-done.1) | data formatting | bytes 1277952 | tf_op jit(solution)/shard_map/reshape | solution.py:152
  13.4 0.2 multiply_reduce_fusion
  13.7 0.1 copy.21
  13.8 0.1 reshape.93.gain_ref
  13.9 1.3 %pad.4.filters_ref = f32[104,4,640]{2,1,0:T(4,128)S(1)} pad(f32[104,4,512]{2,1,0:T(4,128)} %reshape.89, f32[]{:T(128)} %constant.13.clone.1), padding=0_0x0_0x0_128 | pad | bytes 1916932 | tf_op jit(solution)/shard_map/jit(_pad)/pad | solution.py:152
  15.2 0.1 convert_reduce_fusion.1.start_ref
  15.4 0.2 convert_reduce_fusion
  15.5 0.1 select_reduce_fusion.order_ref
  15.6 11.6 %all-to-all-done = bf16[8,4,8704]{2,1,0:T(4,128)(2,1)} async-done(((bf16[8,4,8704]{2,1,0:T(4,128)(2,1)}), bf16[8,4,8704]{2,1,0:T(4,128)(2,1)}, u32[]{:S(2)}, u32[]{:S(2)}) %all-to-all-start) | async-done | bytes 557088 | tf_op jit(solution)/shard_map/all_to_all | solution.py:217
  27.2 1.5 %reshape.100.lanes_ref = bf16[8,4,68,128]{3,2,1,0:T(8,128)(2,1)S(1)} reshape(bf16[8,4,8704]{2,1,0:T(4,128)(2,1)} %all-to-all-done) | data formatting | bytes 1114112 | tf_op jit(solution)/shard_map/reshape | solution.py:149
  28.7 21.1 %correlate.1 = (f32[2,52,16,128]{3,2,1,0:T(8,128)S(1)}, f32[2,52,16,128]{3,2,1,0:T(8,128)S(1)}) custom-call(s32[1]{0:T(128)} %bitcast.me_ref, s32[9]{0:T(128)S(1)} %convert_reduce_fusion.1.start_ref, s32[121]{0:T(128)S(1)} %select_reduce_fusion.order_ref, f32[416]{0:T(512)S(1)} %reshape.93.gain_ref, bf16[256,128]{1,0:T(8,128)(2,1)S(1)} %add_convert_fusion.steps_ref, ...), custom_call_target="tpu_custom_call" | custom-call | tf_op jit(solution)/shard_map/correlate/pallas_call | solution.py:173
  49.9 2.4 %collective-permute-done = f32[2,52,16,128]{3,2,1,0:T(8,128)S(1)} collective-permute-done((f32[2,52,16,128]{3,2,1,0:T(8,128)S(1)}, f32[2,52,16,128]{3,2,1,0:T(8,128)S(1)}, u32[]{:S(2)}, u32[]{:S(2)}) %collective-permute-start) | collective-permute-done | bytes 852000 | tf_op jit(solution)/shard_map/ppermute | solution.py:201
  52.3 0.1 add_bitcast_fusion
  52.4 1.6 %collective-permute-start.1 = (f32[1,52,16,128]{3,2,1,0:T(8,128)S(1)}, f32[1,52,16,128]{3,2,1,0:T(8,128)S(1)}, u32[]{:S(2)}, u32[]{:S(2)}) collective-permute-start(f32[1,52,16,128]{3,2,1,0:T(8,128)S(1)} %slice_bitcast_fusion), channel_id=1, source_target_pairs={{0,2},{1,3},{2,0},{3,1},{4,6},{5,7},{6,4},{7,5},{8,10},{9,11},{10,... | collective-permute-start | bytes 1277960 | tf_op jit(solution)/shard_map/ppermute | solution.py:201
  54.0 10.3 %collective-permute-done.1 = f32[1,52,16,128]{3,2,1,0:T(8,128)S(1)} collective-permute-done((f32[1,52,16,128]{3,2,1,0:T(8,128)S(1)}, f32[1,52,16,128]{3,2,1,0:T(8,128)S(1)}, u32[]{:S(2)}, u32[]{:S(2)}) %collective-permute-start.1) | collective-permute-done | bytes 426016 | tf_op jit(solution)/shard_map/ppermute | solution.py:201
  64.4 0.9 %copy.26 = f32[7,8,16,128]{3,1,2,0:T(8,128)} copy(f32[7,8,16,128]{3,2,1,0:T(8,128)S(1)} %bitcast.20) | data formatting | bytes 917504
  (16 shorter events, 0.4 us)
Async XLA Ops:
  0.0 1.5 %copy-start = (bf16[32,3,8704]{2,0,1:T(8,128)(2,1)S(1)}, bf16[32,3,8704]{2,0,1:T(8,128)(2,1)}, u32[]{:S(2)}) copy-start(bf16[32,3,8704]{2,0,1:T(8,128)(2,1)} %param.4) | copy-start | bytes 5013508
  3.7 8.2 %copy-start.2 = (s32[1,416,2]{1,2,0:T(2,128)S(1)}, s32[1,416,2]{1,2,0:T(2,128)}, u32[]{:S(2)}) copy-start(s32[1,416,2]{1,2,0:T(2,128)} %param.6) | copy-start | bytes 9988
  3.7 8.5 %copy-start.1 = (bf16[52,8,512]{2,1,0:T(8,128)(2,1)S(1)}, bf16[52,8,512]{2,1,0:T(8,128)(2,1)}, u32[]{:S(2)}) copy-start(bf16[52,8,512]{2,1,0:T(8,128)(2,1)} %param.5) | copy-start | bytes 1277956
  4.6 22.5 %all-to-all-start = ((bf16[8,4,8704]{2,1,0:T(4,128)(2,1)}), bf16[8,4,8704]{2,1,0:T(4,128)(2,1)}, u32[]{:S(2)}, u32[]{:S(2)}) async-start(bf16[8,4,8704]{2,1,0:T(4,128)(2,1)} %reshape.87), calls=%async_computation | async-start | bytes 1114112 | tf_op jit(solution)/shard_map/all_to_all | solution.py:217
  49.8 2.4 %collective-permute-start = (f32[2,52,16,128]{3,2,1,0:T(8,128)S(1)}, f32[2,52,16,128]{3,2,1,0:T(8,128)S(1)}, u32[]{:S(2)}, u32[]{:S(2)}) collective-permute-start(f32[2,52,16,128]{3,2,1,0:T(8,128)S(1)} %get-tuple-element.8), channel_id=1, source_target_pairs={{0,1},{1,0},{2,3},{3,2},{4,5},{5,4},{6,7},{7,6},{8,9},{9,8},{10,11... | collective-permute-start | bytes 2555912 | tf_op jit(solution)/shard_map/ppermute | solution.py:201
  52.4 11.9 %collective-permute-start.1 = (f32[1,52,16,128]{3,2,1,0:T(8,128)S(1)}, f32[1,52,16,128]{3,2,1,0:T(8,128)S(1)}, u32[]{:S(2)}, u32[]{:S(2)}) collective-permute-start(f32[1,52,16,128]{3,2,1,0:T(8,128)S(1)} %slice_bitcast_fusion), channel_id=1, source_target_pairs={{0,2},{1,3},{2,0},{3,1},{4,6},{5,7},{6,4},{7,5},{8,10},{9,11},{10,... | collective-permute-start | bytes 1277960 | tf_op jit(solution)/shard_map/ppermute | solution.py:201
